TPU v7x, 512 devices: a whole 4x4x16 slice. The times are simulated.
512 devices in a mesh: member: 16 (over z), space: 32 (over y, x, core).
Axes of the slice: x: 4, y: 4, z: 16, core: 2. Of those that a mesh axis runs over, the one named last changes fastest.
Arguments:
- coarse_state: float32 [16, 3, 2048, 512], P('member', None, 'space'), may hold values from -6 to 6
- coarse_seabed: float32 [2048, 512], P('space'), may hold values from 0.2 to 1
- open_faces: int32 [2, 2048, 512], P(None, 'space'), may hold values 0 or 1
- fine_state: float32 [16, 3, 192, 128, 128], P('member', None, 'space'), may hold values from -6 to 6
- fine_seabed: float32 [192, 128, 128], P('space'), may hold values from 0.2 to 1
- slot_patch: int32 [192], replicated, may hold values from -1 to 63, as said below
- patch_anchor: int32 [64, 2], replicated, may hold values from 1 to 479, as said below
- gauge_cells: int32 [128], replicated, may hold values from 0 to 1048575
Outputs:
- coarse_out: float32 [16, 3, 2048, 512], P('member', None, 'space')
- fine_out: float32 [16, 3, 192, 128, 128], P('member', None, 'space')
- gauge_spread: float32 [16, 128], P('member')
Inputs may be any that keep to these rules, and one draw needn't show every extreme that they name: `slot_patch`: every patch stands in exactly one slot; occupied slots of an owner come first; a quarter of the owners hold 6 patches, half hold one and a quarter none; no owner holds two patches with the same parent slab; empty slots hold -1. `patch_anchor`: entry [p, 0] lies in 1 .. 31; entry [p, 1] lies in 1 .. 223 for even p and in 257 .. 479 for odd p.
All inputs are finite; a program needn't handle non-finite values. No bound on the sum of `open_faces` on one device may be relied on, other than what follows from the above.
Results may differ from a plain program's by a relative error of at most 0.0003.
Values sent between devices are 32-bit elements; how exact they have to be, the bound alone decides.
A program may use at most 64 MiB of HBM per device.

v0:
```python
import jax
import jax.numpy as jnp
from jax import lax
from jax.sharding import PartitionSpec as P

REFINE = 4
STEPS = 2


courant = 0.5


def from_behind(value, axis, steps):
    count = lax.axis_size(axis)
    leading, last = (max(0, -steps), min(count, count - steps))
    return lax.ppermute(value, axis, [(source, source + steps) for source in range(leading, last)])


def coarse_advance(fields, seabed, open_faces):
    height = fields[:, 0]
    east_flux = fields[:, 1]
    north_flux = fields[:, 2]
    zero_column = jnp.zeros_like(height[..., :1])
    west_flux = jnp.concatenate([zero_column, east_flux[..., :-1]], axis=-1)
    below_row = from_behind(north_flux[:, -1, :], "space", 1)
    south_flux = jnp.concatenate([below_row[:, None, :], north_flux[:, :-1, :]], axis=1)
    height_new = height - courant * (east_flux - west_flux + north_flux - south_flux)
    above_row = from_behind(height_new[:, 0, :], "space", -1)
    height_up = jnp.concatenate([height_new[:, 1:, :], above_row[:, None, :]], axis=1)
    height_right = jnp.concatenate([height_new[..., 1:], zero_column], axis=-1)
    open_east = open_faces[0].astype(jnp.float32)
    open_north = open_faces[1].astype(jnp.float32)
    east_new = open_east * (east_flux - courant * seabed * (height_right - height_new))
    north_new = open_north * (north_flux - courant * seabed * (height_up - height_new))
    return jnp.stack([height_new, east_new, north_new], axis=1)


def cycle_values(both_times, row_start, col_start, block_len):
    members = both_times.shape[0]
    anchor = jnp.zeros((), jnp.int32)
    row_first = row_start - 1
    col_first = col_start - 1
    region = lax.dynamic_slice(
        both_times,
        (anchor, anchor, anchor, row_first, col_first),
        (members, 2, 3, block_len + 2, block_len + 2),
    )
    west_side = region[:, :, 1, 1 : block_len + 1, 0]
    south_side = region[:, :, 2, 0, 1 : block_len + 1]
    east_side = region[:, :, 0, 1 : block_len + 1, block_len + 1]
    north_side = region[:, :, 0, block_len + 1, 1 : block_len + 1]
    return jnp.concatenate([west_side, south_side, east_side, north_side], axis=-1)


def fine_advance(fine_fields, fine_seabed, ghosts, refine):
    height = fine_fields[:, 0]
    east_flux = fine_fields[:, 1]
    north_flux = fine_fields[:, 2]
    fine_len = height.shape[-1]
    spread = jnp.repeat(ghosts, refine, axis=-1)
    old_edges = spread[:, :, 0]
    new_edges = spread[:, :, 1]
    for substep in range(refine):
        flux_weight = (2 * substep + 1) / (2.0 * refine)
        level_weight = (substep + 1) / float(refine)
        flux_edge = old_edges + flux_weight * (new_edges - old_edges)
        level_edge = old_edges + level_weight * (new_edges - old_edges)
        west_edge = flux_edge[..., 0:fine_len]
        south_edge = flux_edge[..., fine_len : 2 * fine_len]
        east_edge = level_edge[..., 2 * fine_len : 3 * fine_len]
        north_edge = level_edge[..., 3 * fine_len : 4 * fine_len]
        west_flux = jnp.concatenate([west_edge[..., :, None], east_flux[..., :-1]], axis=-1)
        south_flux = jnp.concatenate([south_edge[..., None, :], north_flux[..., :-1, :]], axis=-2)
        height = height - courant * (east_flux - west_flux + north_flux - south_flux)
        height_right = jnp.concatenate([height[..., 1:], east_edge[..., :, None]], axis=-1)
        height_up = jnp.concatenate([height[..., 1:, :], north_edge[..., None, :]], axis=-2)
        east_flux = east_flux - courant * fine_seabed * (height_right - height)
        north_flux = north_flux - courant * fine_seabed * (height_up - height)
    return jnp.stack([height, east_flux, north_flux], axis=1)


def block_average(fine_fields, block_len, refine):
    members = fine_fields.shape[0]
    slot_count = fine_fields.shape[2]
    height_means = (
        fine_fields[:, 0]
        .reshape(members, slot_count, block_len, refine, block_len, refine)
        .mean(axis=(3, 5))
    )
    east_means = (
        fine_fields[:, 1][..., refine - 1 :: refine]
        .reshape(members, slot_count, block_len, refine, block_len)
        .mean(axis=3)
    )
    north_means = (
        fine_fields[:, 2][..., refine - 1 :: refine, :]
        .reshape(members, slot_count, block_len, block_len, refine)
        .mean(axis=4)
    )
    return jnp.stack([height_means, east_means, north_means], axis=1)


def shards(
    coarse_state,
    coarse_seabed,
    open_faces,
    fine_state,
    fine_seabed,
    slot_patch,
    patch_anchor,
    gauge_cells,
):
    spaces = lax.axis_size("space")
    position = lax.axis_index("space")
    members = coarse_state.shape[0]
    slab_rows = coarse_state.shape[2]
    slab_cols = coarse_state.shape[3]
    slot_count = fine_state.shape[2]
    block_len = fine_state.shape[-1] // REFINE
    per_slab = patch_anchor.shape[0] // spaces
    anchor = jnp.zeros((), jnp.int32)
    my_patches = position * per_slab + jnp.arange(per_slab, dtype=jnp.int32)
    anchors = lax.dynamic_slice_in_dim(patch_anchor, position * per_slab, per_slab, 0)
    owner_table = slot_patch.reshape(spaces, slot_count)
    holder = jnp.any(owner_table[:, :, None] == my_patches[None, None, :], axis=1).astype(
        jnp.float32
    )
    my_slots = lax.dynamic_slice_in_dim(slot_patch, position * slot_count, slot_count, 0)
    occupied = (my_slots >= 0).astype(jnp.float32)
    sources = (
        my_slots[:, None] // per_slab == jnp.arange(spaces, dtype=jnp.int32)[None, :]
    ).astype(jnp.float32) * occupied[:, None]
    fields = coarse_state
    fine_fields = fine_state * occupied[None, None, :, None, None]
    for step_index in range(STEPS):
        advanced = coarse_advance(fields, coarse_seabed, open_faces)
        both_times = jnp.stack([fields, advanced], axis=1)
        cycle_stack = jnp.stack(
            [
                cycle_values(
                    both_times, anchors[patch_index, 0], anchors[patch_index, 1], block_len
                )
                for patch_index in range(per_slab)
            ],
            axis=0,
        )
        cycle_rows = cycle_stack.reshape(per_slab, -1)
        outgoing = jnp.sum(holder[:, :, None] * cycle_rows[None], axis=1)
        incoming = lax.all_to_all(outgoing, "space", split_axis=0, concat_axis=0, tiled=True)
        ghosts = jnp.sum(sources[:, :, None] * incoming[None], axis=1)
        ghosts = jnp.transpose(ghosts.reshape(slot_count, members, 2, 4 * block_len), (1, 0, 2, 3))
        fine_fields = (
            fine_advance(fine_fields, fine_seabed, ghosts, REFINE)
            * occupied[None, None, :, None, None]
        )
        averages = block_average(fine_fields, block_len, REFINE)
        mean_rows = jnp.transpose(averages, (2, 0, 1, 3, 4)).reshape(slot_count, -1)
        outgoing = jnp.sum(jnp.transpose(sources)[:, :, None] * mean_rows[None], axis=1)
        incoming = lax.all_to_all(outgoing, "space", split_axis=0, concat_axis=0, tiled=True)
        patch_means = jnp.sum(jnp.transpose(holder)[:, :, None] * incoming[None], axis=1)
        patch_means = patch_means.reshape(per_slab, members, 3, block_len, block_len)
        for patch_index in range(per_slab):
            advanced = lax.dynamic_update_slice(
                advanced,
                patch_means[patch_index],
                (anchor, anchor, anchors[patch_index, 0], anchors[patch_index, 1]),
            )
        fields = advanced
    slab_cells = slab_rows * slab_cols
    local_cell = gauge_cells - position * slab_cells
    inside = ((local_cell >= 0) & (local_cell < slab_cells)).astype(jnp.float32)
    readings = (
        jnp.take(
            fields[:, 0].reshape(members, slab_cells),
            jnp.clip(local_cell, 0, slab_cells - 1),
            axis=1,
        )
        * inside[None, :]
    )
    member_place = lax.axis_index("member") * members
    everyone = jnp.zeros((members * lax.axis_size("member"), readings.shape[1]), jnp.float32)
    everyone = lax.dynamic_update_slice(everyone, readings, (member_place, anchor))
    totals = lax.psum(everyone, ("member", "space"))
    member_count = totals.shape[0]
    weights = 1.0 + 2.0 * jnp.arange(member_count, dtype=jnp.float32) / (member_count - 1)
    weights = weights / jnp.sum(weights)
    center = jnp.sum(weights[:, None] * totals, axis=0)
    own_rows = lax.dynamic_slice_in_dim(totals, member_place, members, 0)
    return (fields, fine_fields, own_rows - center[None, :])


def solution(mesh):
    return jax.shard_map(
        shards,
        mesh=mesh,
        in_specs=(
            P("member", None, "space", None),
            P("space", None),
            P(None, "space", None),
            P("member", None, "space", None, None),
            P("space", None, None),
            P(),
            P(),
            P(),
        ),
        out_specs=(
            P("member", None, "space", None),
            P("member", None, "space", None, None),
            P("member", None),
        ),
        check_vma=False,
    )
```

profile of v0, /device:TPU:1, one launch (start us, length us, event | category | flops | bytes accessed | tf_op | source)
XLA Modules:
  0.0 303.4 jit_solution(16441541458864858202)
XLA Ops:
  1.7 4.5 %collective-permute-start = (f32[1,512]{1,0:T(1,128)S(1)}, f32[1,512]{1,0:T(1,128)S(1)}, u32[]{:S(2)}, u32[]{:S(2)}) collective-permute-start(f32[1,512]{1,0:T(1,128)S(1)} %slice_bitcast_fusion.75), channel_id=1, source_target_pairs={{0,1},{1,2},{2,3},{3,4},{4,5},{5,6},{6,7},{7,8},{8,9},{9,10},{10,1... | collective-permute-start | bytes 6152 | tf_op jit(solution)/shard_map/ppermute | solution.py:16
  12.1 5.6 %collective-permute-start.1 = (f32[1,512]{1,0:T(1,128)S(1)}, f32[1,512]{1,0:T(1,128)S(1)}, u32[]{:S(2)}, u32[]{:S(2)}) collective-permute-start(f32[1,512]{1,0:T(1,128)S(1)} %slice_bitcast_fusion.74), channel_id=1, source_target_pairs={{1,0},{2,1},{3,2},{4,3},{5,4},{6,5},{7,6},{8,7},{9,8},{10,9},{11,1... | collective-permute-start | bytes 6152 | tf_op jit(solution)/shard_map/ppermute | solution.py:16
  24.9 4.1 %all-to-all-start = ((f32[32,1,256]{2,1,0:T(1,128)}), f32[32,1,256]{2,1,0:T(1,128)S(1)}, u32[]{:S(2)}, u32[]{:S(2)}) async-start(f32[32,1,256]{2,1,0:T(1,128)} %copy.181), calls=%async_computation | async-start | bytes 65536 | tf_op jit(solution)/shard_map/all_to_all | solution.py:149
  29.1 7.2 %all-to-all-done = f32[32,1,256]{2,1,0:T(1,128)S(1)} async-done(((f32[32,1,256]{2,1,0:T(1,128)}), f32[32,1,256]{2,1,0:T(1,128)S(1)}, u32[]{:S(2)}, u32[]{:S(2)}) %all-to-all-start) | async-done | bytes 32800 | tf_op jit(solution)/shard_map/all_to_all | solution.py:149
  56.4 14.3 %reshape_squeeze.9 = f32[6,32,4,32,4]{4,3,2,1,0:T(8,128)} reshape(f32[1,1,6,128,128]{4,3,2,1,0:T(8,128)S(1)} %get-tuple-element.29) | data formatting | bytes 786432 | tf_op jit(solution)/shard_map/reshape;squeeze | solution.py:87
  70.8 5.6 %reduce_sum.146 = f32[6,32,32]{2,1,0:T(8,128)S(1)} reduce(f32[6,32,4,32,4]{4,3,2,1,0:T(8,128)} %reshape_squeeze.9, f32[]{:T(128)} %constant.36.clone.1), dimensions={2,4}, to_apply=%region_3.4 | reduce | flops 92160 | bytes 417796 | tf_op jit(solution)/shard_map/reduce_sum | solution.py:88
  77.0 3.6 %slice.461 = f32[1,6,128,32]{3,2,1,0:T(8,128)S(1)} slice(f32[1,6,128,128]{3,2,1,0:T(8,128)S(1)} %get-tuple-element.31), slice={[0:1:1], [0:6:1], [0:128:1], [3:128:4]} | slice | bytes 196608 | tf_op jit(solution)/shard_map/slice | solution.py:91
  82.4 3.9 %all-to-all-start.1 = ((f32[32,1,3072]{2,1,0:T(1,128)}), f32[32,1,3072]{2,1,0:T(1,128)S(1)}, u32[]{:S(2)}, u32[]{:S(2)}) async-start(f32[32,1,3072]{2,1,0:T(1,128)} %copy.196), calls=%async_computation.1 | async-start | bytes 786432 | tf_op jit(solution)/shard_map/all_to_all | solution.py:159
  93.8 2.8 all-to-all-done.1
  97.1 1.7 dynamic_update_slice.15
  98.8 1.7 dynamic_update_slice.16
  100.6 2.5 collective-permute-start.2
  103.9 2.1 collective-permute-start.3
  106.9 2.5 collective-permute-done.3
  111.9 7.3 %all-to-all-start.2 = ((f32[32,1,256]{2,1,0:T(1,128)}), f32[32,1,256]{2,1,0:T(1,128)S(1)}, u32[]{:S(2)}, u32[]{:S(2)}) async-start(f32[32,1,256]{2,1,0:T(1,128)} %copy.197), calls=%async_computation.2 | async-start | bytes 65536 | tf_op jit(solution)/shard_map/all_to_all | solution.py:149
  120.0 6.4 %all-to-all-done.2 = f32[32,1,256]{2,1,0:T(1,128)S(1)} async-done(((f32[32,1,256]{2,1,0:T(1,128)}), f32[32,1,256]{2,1,0:T(1,128)S(1)}, u32[]{:S(2)}, u32[]{:S(2)}) %all-to-all-start.2) | async-done | bytes 32800 | tf_op jit(solution)/shard_map/all_to_all | solution.py:149
  146.2 14.3 %reshape_squeeze.10 = f32[6,32,4,32,4]{4,3,2,1,0:T(8,128)} reshape(f32[1,1,6,128,128]{4,3,2,1,0:T(8,128)S(1)} %get-tuple-element.26) | data formatting | bytes 786432 | tf_op jit(solution)/shard_map/reshape;squeeze | solution.py:87
  160.5 5.6 %reduce_sum.153 = f32[6,32,32]{2,1,0:T(8,128)S(1)} reduce(f32[6,32,4,32,4]{4,3,2,1,0:T(8,128)} %reshape_squeeze.10, f32[]{:T(128)} %constant.36.clone.1), dimensions={2,4}, to_apply=%region_10.11 | reduce | flops 92160 | bytes 417796 | tf_op jit(solution)/shard_map/reduce_sum | solution.py:88
  166.7 3.6 %slice.519 = f32[1,6,128,32]{3,2,1,0:T(8,128)S(1)} slice(f32[1,6,128,128]{3,2,1,0:T(8,128)S(1)} %get-tuple-element.28), slice={[0:1:1], [0:6:1], [0:128:1], [3:128:4]} | slice | bytes 196608 | tf_op jit(solution)/shard_map/slice | solution.py:91
  172.1 3.9 %all-to-all-start.3 = ((f32[32,1,3072]{2,1,0:T(1,128)}), f32[32,1,3072]{2,1,0:T(1,128)S(1)}, u32[]{:S(2)}, u32[]{:S(2)}) async-start(f32[32,1,3072]{2,1,0:T(1,128)} %copy.213), calls=%async_computation.3 | async-start | bytes 786432 | tf_op jit(solution)/shard_map/all_to_all | solution.py:159
  176.8 9.6 %all-to-all-done.3 = f32[32,1,3072]{2,1,0:T(1,128)S(1)} async-done(((f32[32,1,3072]{2,1,0:T(1,128)}), f32[32,1,3072]{2,1,0:T(1,128)S(1)}, u32[]{:S(2)}, u32[]{:S(2)}) %all-to-all-start.3) | async-done | bytes 393248 | tf_op jit(solution)/shard_map/all_to_all | solution.py:159
  186.8 3.3 %dynamic_update_slice.17 = f32[1,3,64,512]{3,2,1,0:T(8,128)} dynamic-update-slice(f32[1,3,64,512]{3,2,1,0:T(8,128)} %get-tuple-element.59, f32[1,3,32,32]{3,2,1,0:T(8,128)S(1)} %squeeze.218, s32[]{:T(128)} %constant.44.clone.1, s32[]{:T(128)} %constant.44.clone.1, s32[]{:T(128)S(6)} %select_n.65, s32[]{:T(128)S(6)} %select_n.66) | dynamic-update-slice | bytes 24580 | tf_op jit(solution)/shard_map/dynamic_update_slice | solution.py:163
  190.1 3.3 %dynamic_update_slice.18 = f32[1,3,64,512]{3,2,1,0:T(8,128)} dynamic-update-slice(f32[1,3,64,512]{3,2,1,0:T(8,128)} %dynamic_update_slice.17, f32[1,3,32,32]{3,2,1,0:T(8,128)S(1)} %squeeze.219, s32[]{:T(128)} %constant.44.clone.1, s32[]{:T(128)} %constant.44.clone.1, s32[]{:T(128)S(6)} %select_n.67, s32[]{:T(128)S(6)} %select_n.68) | dynamic-update-slice | bytes 24580 | tf_op jit(solution)/shard_map/dynamic_update_slice | solution.py:163
  195.6 107.2 %psum.7 = f32[16,128]{1,0:T(8,128)S(1)} all-reduce(f32[16,128]{1,0:T(8,128)S(1)} %dynamic_update_slice.19), channel_id=1, replica_groups=mesh['member'=16,'space'=32] {'member','space'}, use_global_device_ids=true, to_apply=%region_15.16 | all-reduce | flops 2048 | bytes 16384 | tf_op jit(solution)/shard_map/psum | solution.py:183
  (268 shorter events, 62.4 us)
Async XLA Ops:
  0.6 11.2 %copy-start = (s32[64,2]{0,1:T(2,128)S(1)}, s32[64,2]{0,1:T(2,128)}, u32[]{:S(2)}) copy-start(s32[64,2]{0,1:T(2,128)} %param.14) | copy-start | bytes 1540
  1.7 10.3 %collective-permute-start = (f32[1,512]{1,0:T(1,128)S(1)}, f32[1,512]{1,0:T(1,128)S(1)}, u32[]{:S(2)}, u32[]{:S(2)}) collective-permute-start(f32[1,512]{1,0:T(1,128)S(1)} %slice_bitcast_fusion.75), channel_id=1, source_target_pairs={{0,1},{1,2},{2,3},{3,4},{4,5},{5,6},{6,7},{7,8},{8,9},{9,10},{10,1... | collective-permute-start | bytes 6152 | tf_op jit(solution)/shard_map/ppermute | solution.py:16
  7.7 48.4 %copy-start.24 = (f32[6]{0:T(128)}, f32[6]{0:T(128)S(1)}, u32[]{:S(2)}) copy-start(f32[6]{0:T(128)S(1)} %compare_convert_fusion) | copy-start | bytes 76
  9.2 15.0 %copy-start.31 = (f32[32,2]{0,1:T(2,128)}, f32[32,2]{0,1:T(2,128)S(1)}, u32[]{:S(2)}) copy-start(f32[32,2]{0,1:T(2,128)S(1)} %get-tuple-element.133) | copy-start | bytes 772
  10.9 12.5 %copy-start.8 = (s32[2,64,512]{2,1,0:T(8,128)S(1)}, s32[2,64,512]{2,1,0:T(8,128)}, u32[]{:S(2)}) copy-start(s32[2,64,512]{2,1,0:T(8,128)} %param.10) | copy-start | bytes 786436
  10.9 12.5 %copy-start.10 = (f32[64,512]{1,0:T(8,128)S(1)}, f32[64,512]{1,0:T(8,128)}, u32[]{:S(2)}) copy-start(f32[64,512]{1,0:T(8,128)} %param.9) | copy-start | bytes 393220
  12.1 11.3 %collective-permute-start.1 = (f32[1,512]{1,0:T(1,128)S(1)}, f32[1,512]{1,0:T(1,128)S(1)}, u32[]{:S(2)}, u32[]{:S(2)}) collective-permute-start(f32[1,512]{1,0:T(1,128)S(1)} %slice_bitcast_fusion.74), channel_id=1, source_target_pairs={{1,0},{2,1},{3,2},{4,3},{5,4},{6,5},{7,6},{8,7},{9,8},{10,9},{11,1... | collective-permute-start | bytes 6152 | tf_op jit(solution)/shard_map/ppermute | solution.py:16
  24.9 11.3 %all-to-all-start = ((f32[32,1,256]{2,1,0:T(1,128)}), f32[32,1,256]{2,1,0:T(1,128)S(1)}, u32[]{:S(2)}, u32[]{:S(2)}) async-start(f32[32,1,256]{2,1,0:T(1,128)} %copy.181), calls=%async_computation | async-start | bytes 65536 | tf_op jit(solution)/shard_map/all_to_all | solution.py:149
  39.8 4.2 %copy-start.2 = (f32[6,128,128]{2,1,0:T(8,128)S(1)}, f32[6,128,128]{2,1,0:T(8,128)}, u32[]{:S(2)}) copy-start(f32[6,128,128]{2,1,0:T(8,128)} %param.12) | copy-start | bytes 1179652
  39.8 4.2 %copy-start.5 = (f32[6,127,128]{2,1,0:T(8,128)S(1)}, f32[6,127,128]{2,1,0:T(8,128)}, u32[]{:S(2)}) copy-start(f32[6,127,128]{2,1,0:T(8,128)} %get-tuple-element.64) | copy-start | bytes 1170436
  44.0 1.6 copy-start.6
  44.0 1.7 copy-start.27
  81.2 15.5 %copy-start.29 = (f32[2,32]{1,0:T(2,128)S(1)}, f32[2,32]{1,0:T(2,128)}, u32[]{:S(2)}) copy-start(f32[2,32]{1,0:T(2,128)} %get-tuple-element.132) | copy-start | bytes 772
  82.4 14.2 %all-to-all-start.1 = ((f32[32,1,3072]{2,1,0:T(1,128)}), f32[32,1,3072]{2,1,0:T(1,128)S(1)}, u32[]{:S(2)}, u32[]{:S(2)}) async-start(f32[32,1,3072]{2,1,0:T(1,128)} %copy.196), calls=%async_computation.1 | async-start | bytes 786432 | tf_op jit(solution)/shard_map/all_to_all | solution.py:159
  100.6 3.2 %collective-permute-start.2 = (f32[1,512]{1,0:T(1,128)S(1)}, f32[1,512]{1,0:T(1,128)S(1)}, u32[]{:S(2)}, u32[]{:S(2)}) collective-permute-start(f32[1,512]{1,0:T(1,128)S(1)} %slice_bitcast_fusion.73), channel_id=1, source_target_pairs={{0,1},{1,2},{2,3},{3,4},{4,5},{5,6},{6,7},{7,8},{8,9},{9,10},{10,1... | collective-permute-start | bytes 6152 | tf_op jit(solution)/shard_map/ppermute | solution.py:16
  103.8 5.7 %copy-start.9 = (s32[2,64,512]{2,1,0:T(8,128)S(1)}, s32[2,64,512]{2,1,0:T(8,128)}, u32[]{:S(2)}) copy-start(s32[2,64,512]{2,1,0:T(8,128)} %param.10) | copy-start | bytes 786436
  103.8 5.7 %copy-start.11 = (f32[64,512]{1,0:T(8,128)S(1)}, f32[64,512]{1,0:T(8,128)}, u32[]{:S(2)}) copy-start(f32[64,512]{1,0:T(8,128)} %param.9) | copy-start | bytes 393220
  103.9 5.6 %collective-permute-start.3 = (f32[1,512]{1,0:T(1,128)S(1)}, f32[1,512]{1,0:T(1,128)S(1)}, u32[]{:S(2)}, u32[]{:S(2)}) collective-permute-start(f32[1,512]{1,0:T(1,128)S(1)} %slice_bitcast_fusion.72), channel_id=1, source_target_pairs={{1,0},{2,1},{3,2},{4,3},{5,4},{6,5},{7,6},{8,7},{9,8},{10,9},{11,1... | collective-permute-start | bytes 6152 | tf_op jit(solution)/shard_map/ppermute | solution.py:16
  111.9 14.5 %all-to-all-start.2 = ((f32[32,1,256]{2,1,0:T(1,128)}), f32[32,1,256]{2,1,0:T(1,128)S(1)}, u32[]{:S(2)}, u32[]{:S(2)}) async-start(f32[32,1,256]{2,1,0:T(1,128)} %copy.197), calls=%async_computation.2 | async-start | bytes 65536 | tf_op jit(solution)/shard_map/all_to_all | solution.py:149
  130.8 1.9 copy-start.21
  170.6 6.2 %copy-start.33 = (s32[128]{0:T(128)S(1)}, s32[128]{0:T(128)}, u32[]{:S(2)}) copy-start(s32[128]{0:T(128)} %param.15) | copy-start | bytes 1540
  171.0 15.4 %copy-start.30 = (f32[2,32]{1,0:T(2,128)S(1)}, f32[2,32]{1,0:T(2,128)}, u32[]{:S(2)}) copy-start(f32[2,32]{1,0:T(2,128)} %get-tuple-element.132) | copy-start | bytes 772
  172.1 14.2 %all-to-all-start.3 = ((f32[32,1,3072]{2,1,0:T(1,128)}), f32[32,1,3072]{2,1,0:T(1,128)S(1)}, u32[]{:S(2)}, u32[]{:S(2)}) async-start(f32[32,1,3072]{2,1,0:T(1,128)} %copy.213), calls=%async_computation.3 | async-start | bytes 786432 | tf_op jit(solution)/shard_map/all_to_all | solution.py:159
  176.8 126.7 %copy-start.1 = (s32[64,2]{0,1:T(2,128)S(1)}, s32[64,2]{0,1:T(2,128)}, u32[]{:S(2)}) copy-start(s32[64,2]{0,1:T(2,128)} %param.14) | copy-start | bytes 1540
  (18 other events, 16.2 us)
where the time goes:
time: 306 us; the launch traced here: 303 us
  blocking collectives  107 us (35%)
  local copies, waits for them, and re-layouts  83.4 us (27%)
  other arithmetic  35.9 us (12%)
  starting transfers between devices  33.8 us (11%)
  waiting for transfers between devices  28.6 us (9%)
  between operations  14.5 us (5%)
    psum x1, blocking collectives, shards(): totals = lax.psum(everyone, ('member', 'space'))  107 us
    another operation x2, local copies, waits for them, and re-layouts, block_average(): height_means = fine_fields[:, 0].reshape(members, slot_count, block_len,...  28.7 us
    all_to_all x4, waiting for transfers between devices, shards(): lax.all_to_all(outgoing, 'space', split_axis=0, concat_axis=0, tiled=True)  26 us
    all_to_all x4, starting transfers between devices, shards(): lax.all_to_all(outgoing, 'space', split_axis=0, concat_axis=0, tiled=True)  19.2 us
    ppermute x4, starting transfers between devices, from_behind(): lax.ppermute(value, axis, [(source, source + steps) for source in range(l...  14.6 us
    reduce_sum x2, other arithmetic, block_average(): height_means = fine_fields[:, 0].reshape(members, slot_count, block_len,...  11.2 us
    dynamic_update_slice x4, local copies, waits for them, and re-layouts, shards(): lax.dynamic_update_slice(advanced, patch_means[patch_index], (anchor, anc...  10.1 us
    unnamed x74, local copies, waits for them, and re-layouts  8.61 us
  transfers between devices with their start and end apart: 8, of which 6 were waited for; matrix products, arithmetic and copies ran while one was open for 3% of the time, Pallas kernels for 0%

commit v1 on v0

v1 whole, which is shorter than its diff:
```python
import functools

import jax
import jax.numpy as jnp
from jax import lax
from jax.experimental import pallas as pl
from jax.experimental.pallas import tpu as pltpu
from jax.sharding import PartitionSpec as P

REFINE = 4
C = 0.5
MESH = pl.DeviceIdType.MESH
f32 = jnp.float32
NT = (((1,), (1,)), ((), ()))
NN = (((1,), (0,)), ((), ()))


def dot(a, b, dims=NN):
    return lax.dot_general(
        a, b, dims, precision=lax.Precision.HIGHEST, preferred_element_type=f32
    )


def iota(shape, dim):
    return lax.broadcasted_iota(jnp.int32, shape, dim)


def roll(x, shift, axis):
    return pltpu.roll(x, shift, axis)


def kernel(
    ns, nm, slots,
    slot, anchor, gauge, coarse, seabed, faces, fine, fseabed,
    coarse_out, fine_out, spread_out,
    cs, sd, op, t1, t2, ex, ce, cn, fh, fu, fv, fd,
    up_s, dn_s, up_r, dn_r, rs, pay_s, pay_r, xb, gx, ycol, yrow, red, tp,
    m1_p, m1_s, m1_r, a2_p, a2_s, a2_r, pz, cout, z_s, z_r, g_s, g_r, sidx,
    in_sem, out_sem, send_sem, recv_sem,
):
    me = lax.axis_index("space")
    mem = lax.axis_index("member")
    rows, cols = sd.shape
    fl = fu.shape[-1]
    bl = fl // REFINE
    nb = slots * 8

    loads = [
        pltpu.make_async_copy(coarse.at[0], cs, in_sem.at[0]),
        pltpu.make_async_copy(seabed, sd, in_sem.at[1]),
        pltpu.make_async_copy(faces, op, in_sem.at[2]),
        pltpu.make_async_copy(fine.at[0, 0], fh.at[:, pl.ds(8, fl), :], in_sem.at[3]),
        pltpu.make_async_copy(fine.at[0, 1], fu, in_sem.at[4]),
        pltpu.make_async_copy(fine.at[0, 2], fv.at[:, pl.ds(8, fl), :], in_sem.at[5]),
        pltpu.make_async_copy(fseabed, fd, in_sem.at[6]),
    ]
    for load in loads:
        load.start()

    barrier = pltpu.get_barrier_semaphore()

    def greet_space(k, carry):
        pl.semaphore_signal(
            barrier, inc=1, device_id=(mem, lax.rem(me + k, ns)), device_id_type=MESH
        )
        return carry

    def greet_member(k, carry):
        pl.semaphore_signal(
            barrier, inc=1, device_id=(lax.rem(mem + k, nm), me), device_id_type=MESH
        )
        return carry

    lax.fori_loop(1, ns, greet_space, 0)
    lax.fori_loop(1, nm, greet_member, 0)

    my_patch = [slot[me * slots + s] for s in range(slots)]
    held_parent = [p >> 1 for p in my_patch]

    def find_slot(k, carry):
        d = lax.rem(me + k + 1, ns)
        which = jnp.int32(0)
        for s in range(1, slots):
            which = jnp.where(held_parent[s] == d, s, which)
        sidx[k] = which
        return carry

    lax.fori_loop(0, ns, find_slot, 0)

    def find_owner(i, carry):
        p = slot[i]
        return tuple(
            jnp.where(p == 2 * me + j, i, carry[j]) for j in range(2)
        )

    where_held = lax.fori_loop(0, ns * slots, find_owner, (jnp.int32(0), jnp.int32(0)))
    owner_at = [lax.rem(me - w // slots - 1 + 2 * ns, ns) for w in where_held]
    r0 = [jnp.clip(anchor[0, 2 * me + j], 1, rows - bl - 1) for j in range(2)]
    c0 = [jnp.clip(anchor[1, 2 * me + j], 1, cols - bl - 1) for j in range(2)]

    lane = iota((1, 128), 1)
    row8 = iota((8, 128), 0)
    lane8 = iota((8, 128), 1)
    rowc = iota((rows, cols), 0)
    lanec = iota((rows, cols), 1)
    lane1 = iota((1, cols), 1)
    block = None
    for j in range(2):
        inside = (
            (rowc >= r0[j]) & (rowc < r0[j] + bl) & (lanec >= c0[j]) & (lanec < c0[j] + bl)
        )
        block = inside if block is None else block | inside

    def west(x):
        first = iota(x.shape, 1) == 0
        return jnp.where(first, 0.0, roll(x, 1, 1))

    def east(x):
        last = iota(x.shape, 1) == cols - 1
        return jnp.where(last, 0.0, roll(x, cols - 1, 1))

    def south(x, below):
        return jnp.where(rowc == 0, below, roll(x, 1, 0))

    def north(x, above):
        return jnp.where(rowc == rows - 1, above, roll(x, rows - 1, 0))

    for load in loads[:3]:
        load.wait()
    h0, u0, v0 = cs[0], cs[1], cs[2]
    oe = op[0].astype(f32)
    on = op[1].astype(f32)
    cd = C * sd[...]
    ce[...] = cd * oe
    cn[...] = cd * on
    h1 = h0 - C * (u0 - west(u0) + v0 - south(v0, 0.0))
    t1[0] = h1
    up_s[0:1, :] = h1[rows - 1 : rows]
    up_s[1:2, :] = v0[rows - 1 : rows]
    up_s[2:3, :] = on[rows - 1 : rows]
    up_s[3:4, :] = cn[rows - 1 : rows, :]
    up_s[4:8, :] = jnp.zeros((4, cols), f32)
    dn_s[0:1, :] = h1[0:1]
    dn_s[1:2, :] = u0[0:1]
    dn_s[2:3, :] = v0[0:1]
    dn_s[3:4, :] = h1[1:2]
    dn_s[4:5, :] = oe[0:1]
    dn_s[5:6, :] = ce[0:1, :]
    dn_s[6:7, :] = on[0:1]
    dn_s[7:8, :] = cn[0:1, :]

    pl.semaphore_wait(barrier, ns + nm - 2)

    up = pltpu.make_async_remote_copy(
        src_ref=up_s, dst_ref=up_r, send_sem=send_sem.at[0], recv_sem=recv_sem.at[0],
        device_id=(mem, lax.rem(me + 1, ns)), device_id_type=MESH,
    )
    down = pltpu.make_async_remote_copy(
        src_ref=dn_s, dst_ref=dn_r, send_sem=send_sem.at[1], recv_sem=recv_sem.at[1],
        device_id=(mem, lax.rem(me + ns - 1, ns)), device_id_type=MESH,
    )
    up.start()
    down.start()

    xb[...] = jnp.zeros(xb.shape, f32)
    gx[...] = jnp.zeros(gx.shape, f32)
    tp[...] = jnp.zeros(tp.shape, f32)
    pz[...] = jnp.zeros(pz.shape, f32)
    rs[...] = jnp.zeros(rs.shape, f32)

    up.wait()
    down.wait()

    low = me > 0
    high = me < ns - 1
    h1_m = up_r[0:1, :]
    v0_m = jnp.where(low, up_r[1:2, :], 0.0)
    h1 = jnp.where(rowc == 0, h1 + C * v0_m, h1)
    h1_p = jnp.where(high, dn_r[0:1, :] + C * v0[rows - 1 : rows], 0.0)
    u1 = oe * u0 - ce[...] * (east(h1) - h1)
    v1 = on * v0 - cn[...] * (north(h1, h1_p) - h1)
    u1_p = dn_r[4:5, :] * dn_r[1:2, :] - dn_r[5:6, :] * (east(h1_p) - h1_p)
    v1_p = dn_r[6:7, :] * dn_r[2:3, :] - dn_r[7:8, :] * (dn_r[3:4, :] - h1_p)
    v1_m = jnp.where(
        low, up_r[2:3, :] * v0_m - up_r[3:4, :] * (h1[0:1] - h1_m), 0.0
    )
    h2_p = jnp.where(
        high, h1_p - C * (u1_p - west(u1_p) + v1_p - v1[rows - 1 : rows]), 0.0
    )
    h1 = jnp.where(block, 0.0, h1)
    u1 = jnp.where(block, 0.0, u1)
    v1 = jnp.where(block, 0.0, v1)
    h2 = h1 - C * (u1 - west(u1) + v1 - south(v1, v1_m))
    t1[0], t1[1], t1[2] = h1, u1, v1
    t2[...] = h2
    u2 = oe * u1 - ce[...] * (east(h2) - h2)
    v2 = on * v1 - cn[...] * (north(h2, h2_p) - h2)
    for f, held in enumerate((h0, h1, h2, u0, u1, u2, ce, v0, v1, v2, cn)):
        for tile in range(cols // 128):
            ex[f, tile] = held[:, 128 * tile : 128 * tile + 128]

    payload = None
    for j in range(2):
        cw = c0[j] - 1
        ch = c0[j] + bl
        tw = cw >> 7
        te = ch >> 7
        span = pl.ds(r0[j], bl)
        west_stack = jnp.concatenate(
            [ex[3 + t, tw, span, :] for t in range(4)], axis=0
        )
        east_stack = jnp.concatenate(
            [ex[t, te, span, :] for t in range(3)] + [jnp.full((bl, 128), -1.0, f32)],
            axis=0,
        )
        pick_w = jnp.where((row8 == 1) & (lane8 == (cw & 127)), 1.0, 0.0)
        pick_e = jnp.where((row8 == 0) & (lane8 == (ch & 127)), 1.0, 0.0)
        sides = dot(pick_w, west_stack, NT) + dot(pick_e, east_stack, NT)
        first = c0[j] >> 7
        second = jnp.minimum(first + 1, cols // 128 - 1)
        north_row = pl.ds(r0[j] + bl, 1)
        south_row = pl.ds(r0[j] - 1, 1)
        for t in range(4):
            moved = []
            for half, tile in enumerate((first, second)):
                if t < 3:
                    rs[j, t, half, 2:3, :] = ex[t, tile, north_row, :]
                else:
                    rs[j, t, half, 2:3, :] = jnp.full((1, 128), -1.0, f32)
                rs[j, t, half, 3:4, :] = ex[7 + t, tile, south_row, :]
                moved.append(roll(rs[j, t, half], (32 * t - c0[j]) & 127, 1))
            kept = lane8 - 32 * t < 128 - (c0[j] & 127)
            picked = jnp.where(kept, moved[0], moved[1])
            here = (row8 >= 2) & (row8 < 4) & (lane8 >= 32 * t) & (lane8 < 32 * t + 32)
            sides = jnp.where(here, picked, sides)
        sides = jnp.where(row8 < 4, sides, 0.0)
        payload = sides if j == 0 else payload + roll(sides, 4, 0)
    pay_s[...] = payload
    pay_r[ns - 1] = payload

    def spread_payload(k, carry):
        pltpu.make_async_remote_copy(
            src_ref=pay_s, dst_ref=pay_r.at[k], send_sem=send_sem.at[2],
            recv_sem=recv_sem.at[2], device_id=(mem, lax.rem(me + k + 1, ns)),
            device_id_type=MESH,
        ).start()
        return carry

    lax.fori_loop(0, ns - 1, spread_payload, 0)

    def all_of(ref, count, sem):
        part = ref.at[pl.ds(0, count)]
        pltpu.make_async_copy(part, part, sem).wait()

    rc_i = iota((fl, 128), 0)
    rc_l = iota((fl, 128), 1)
    spread_rows = jnp.where((rc_l & 31) == (rc_i >> 2), 1.0, 0.0)
    spread_lanes = jnp.where((rc_i & 31) == (rc_l >> 2), 1.0, 0.0)
    mean_h = jnp.where((rc_i >> 2) == rc_l, 0.25, 0.0)
    mean_u = jnp.where(rc_i == 4 * (rc_l - 32) + 3, 1.0, 0.0)
    mean_v = jnp.where((rc_i >> 2) == rc_l - 64, 0.25, 0.0)
    lane_nb = iota((nb, 128), 1)

    def expand(old, diff):
        both = jnp.concatenate([old, diff], axis=0)
        ycol[:, 0 : 2 * nb] = dot(spread_rows, both, NT)
        yrow[...] = dot(both, spread_lanes)

    def fine_steps(last):
        lane_f = iota((fl, 128), 1)

        def one_slot(s, carry):
            ego = roll(ycol[...], 127 - 8 * s, 1)
            egd = roll(ycol[...], lax.rem(255 - 8 * s - nb, 128), 1)
            n_old = yrow[pl.ds(8 * s + 2, 1), :]
            s_old = yrow[pl.ds(8 * s + 3, 1), :]
            n_dif = yrow[pl.ds(nb + 8 * s + 2, 1), :]
            s_dif = yrow[pl.ds(nb + 8 * s + 3, 1), :]
            cdf = C * fd[s]
            used = slot[me * slots + s] >= 0
            for k in range(REFINE):
                wf = (2 * k + 1) / (2.0 * REFINE)
                wl = (k + 1) / float(REFINE)
                edge = ego + jnp.where(lane == fl - 1, wl, wf) * egd
                u = fu[s]
                fv[s, 7:8, :] = s_old + wf * s_dif
                v = fv[s, 8 : 8 + fl, :]
                v_s = fv[s, 7 : 7 + fl, :]
                u_w = jnp.where(lane_f == 0, edge, roll(u, 1, 1))
                h = fh[s, 8 : 8 + fl, :] - C * (u - u_w + v - v_s)
                fh[s, 8 : 8 + fl, :] = h
                fh[s, 8 + fl : 9 + fl, :] = n_old + wl * n_dif
                h_e = jnp.where(lane_f == fl - 1, edge, roll(h, fl - 1, 1))
                h_n = fh[s, 9 : 9 + fl, :]
                u = u - cdf * (h_e - h)
                v = v - cdf * (h_n - h)
                if last and k == REFINE - 1:
                    fh[s, 8 : 8 + fl, :] = jnp.where(used, h, 0.0)
                    u = jnp.where(used, u, 0.0)
                    v = jnp.where(used, v, 0.0)
                fu[s] = u
                fv[s, 8 : 8 + fl, :] = v
            return carry

        lax.fori_loop(0, slots, one_slot, 0)

    def averages():
        for s in range(slots):
            span = slice(bl * s, bl * s + bl)
            parts = [fh[s, pl.ds(8 + i, bl, stride=4), :] for i in range(REFINE)]
            red[0, span, :] = 0.25 * ((parts[0] + parts[1]) + (parts[2] + parts[3]))
            parts = [fu[s, pl.ds(i, bl, stride=4), :] for i in range(REFINE)]
            red[1, span, :] = 0.25 * ((parts[0] + parts[1]) + (parts[2] + parts[3]))
            red[2, span, :] = fv[s, pl.ds(11, bl, stride=4), :]
        return dot(red[0], mean_h) + dot(red[1], mean_u) + dot(red[2], mean_v)

    for load in loads[3:]:
        load.wait()
    all_of(pay_r, ns - 1, recv_sem.at[2])

    for s in range(slots):
        p = jnp.maximum(my_patch[s], 0)
        at = lax.rem(me - (p >> 1) - 1 + 2 * ns, ns)
        got = pay_r[at, pl.ds((p & 1) * 4, 4), :]
        xb[8 * s : 8 * s + 4, :] = jnp.where(my_patch[s] >= 0, got, 0.0)

    x = xb[...]
    left = lane_nb < 32
    expand(
        jnp.where(left, x, 0.0), jnp.where(left, roll(x, 96, 1) - x, 0.0)
    )
    fine_steps(False)

    mean = averages()
    pick_i = iota((16, 128), 0)
    pick_l = iota((16, 128), 1)
    pick = jnp.where((pick_i == 0) & (pick_l == 63), C, 0.0)
    pick = pick + jnp.where((pick_i == 1) & (pick_l == 0), 1.0, 0.0)
    pick = pick - jnp.where((pick_i == 1) & ((pick_l == 32) | (pick_l == 64)), C, 0.0)
    pick = pick + jnp.where((pick_i == 9) & (pick_l == 64), C, 0.0)
    for s in range(slots):
        tp[s, 64:96, :] = mean[bl * s : bl * s + bl]
    for s in range(slots):
        side = dot(pick, tp[s], NT)
        side = side[0:8] + roll(side[8:16], 1, 1)
        gx[8 * s : 8 * s + 2, :] = side[0:2]
        top = tp[s, 95:96, :]
        low_row = tp[s, 64:65, :]
        gx[8 * s + 2 : 8 * s + 3, :] = C * top
        gx[8 * s + 3 : 8 * s + 4, :] = roll(low_row, 64, 1) - C * (
            roll(low_row, 32, 1) - jnp.where(lane > 64, roll(low_row, 33, 1), 0.0) + low_row
        )
    new = x - roll(x, 96, 1) * gx[...]
    mid = (lane_nb >= 64) & (lane_nb < 96)
    expand(
        jnp.where((lane_nb >= 32) & (lane_nb < 64), x, 0.0),
        jnp.where(mid, new - roll(x, 32, 1), 0.0),
    )
    packed = jnp.zeros((nb, 128), f32)
    row_nb = iota((nb, 128), 0) & 7
    for q in range(4):
        here = (row_nb == q) & (lane_nb >= 32 * q) & (lane_nb < 32 * q + 32)
        packed = jnp.where(here, roll(new, (32 * q + 64) % 128, 1), packed)
    for s in range(slots):
        m1_p[s] = jnp.sum(packed[8 * s : 8 * s + 8], axis=0, keepdims=True)

    def send_cycle(k, carry):
        m1_s[k] = m1_p[sidx[k]]
        pltpu.make_async_remote_copy(
            src_ref=m1_s.at[k], dst_ref=m1_r.at[k], send_sem=send_sem.at[3],
            recv_sem=recv_sem.at[3], device_id=(mem, lax.rem(me + k + 1, ns)),
            device_id_type=MESH,
        ).start()
        return carry

    lax.fori_loop(0, ns - 1, send_cycle, 0)
    m1_r[ns - 1] = m1_p[sidx[ns - 1]]

    fine_steps(True)
    stores = [
        pltpu.make_async_copy(fh.at[:, pl.ds(8, fl), :], fine_out.at[0, 0], out_sem.at[0]),
        pltpu.make_async_copy(fu, fine_out.at[0, 1], out_sem.at[1]),
        pltpu.make_async_copy(fv.at[:, pl.ds(8, fl), :], fine_out.at[0, 2], out_sem.at[2]),
    ]

    mean = averages()
    for s in range(slots):
        tail = mean[bl * s + 24 : bl * s + 32]
        for i in range(3):
            piece = mean[bl * s + 8 * i : bl * s + 8 * i + 8]
            a2_p[s, 8 * i : 8 * i + 8, :] = jnp.where(
                lane8 < 96, piece, roll(tail, 96 - 32 * i, 1)
            )

    def send_mean(k, carry):
        a2_s[k] = a2_p[sidx[k]]
        pltpu.make_async_remote_copy(
            src_ref=a2_s.at[k], dst_ref=a2_r.at[k], send_sem=send_sem.at[4],
            recv_sem=recv_sem.at[4], device_id=(mem, lax.rem(me + k + 1, ns)),
            device_id_type=MESH,
        ).start()
        return carry

    lax.fori_loop(0, ns - 1, send_mean, 0)
    a2_r[ns - 1] = a2_p[sidx[ns - 1]]
    for store in stores:
        store.start()

    all_of(m1_r, ns - 1, recv_sem.at[3])
    rowh = iota((rows, 128), 0)
    laneh = iota((rows, 128), 1)
    h2 = t2[...]
    fixes = []
    for j in range(2):
        got = m1_r[owner_at[j]]
        match = (laneh & 31) == rowh - r0[j]
        rows_in = (rowc >= r0[j]) & (rowc < r0[j] + bl)
        cols_in = (lanec >= c0[j]) & (lanec < c0[j] + bl)
        east_col = jnp.sum(
            jnp.where(match & (laneh < 32), got, 0.0), axis=1, keepdims=True
        )
        west_col = jnp.sum(
            jnp.where(match & (laneh >= 32) & (laneh < 64), got, 0.0), axis=1, keepdims=True
        )
        got8 = jnp.broadcast_to(got, (8, 128))
        north_row = roll(got8, (c0[j] - 64) & 127, 1)[0:1]
        south_row = roll(got8, (c0[j] - 96) & 127, 1)[0:1]
        north_row = jnp.concatenate([north_row] * (cols // 128), axis=1)
        south_row = jnp.concatenate([south_row] * (cols // 128), axis=1)
        h2 = jnp.where(rows_in & (lanec == c0[j] + bl), east_col, h2)
        h2 = jnp.where(cols_in & (rowc == r0[j] + bl), north_row, h2)
        fixes.append((rows_in & (lanec == c0[j] - 1), west_col,
                      cols_in & (rowc == r0[j] - 1), south_row))
    u1, v1 = t1[1], t1[2]
    u2 = oe * u1 - ce[...] * (east(h2) - h2)
    v2 = on * v1 - cn[...] * (north(h2, h2_p) - h2)
    for at_west, west_col, at_south, south_row in fixes:
        u2 = jnp.where(at_west, west_col, u2)
        v2 = jnp.where(at_south, south_row, v2)
    cout[0], cout[1], cout[2] = h2, u2, v2

    cell = gauge[...]
    grow = cell // cols
    gcol = cell - grow * cols
    own_row = grow - me * rows
    in_block = None
    for j in range(2):
        hit = (
            (own_row >= r0[j]) & (own_row < r0[j] + bl) & (gcol >= c0[j]) & (gcol < c0[j] + bl)
        )
        in_block = hit if in_block is None else in_block | hit
    pick_col = jnp.where(iota((cols, 128), 0) == gcol, 1.0, 0.0)
    found = dot(h2, pick_col)
    value = jnp.sum(
        jnp.where((rowh == own_row) & jnp.logical_not(in_block), found, 0.0),
        axis=0, keepdims=True,
    )
    rel_col = jnp.full((1, 128), -1, jnp.int32)
    rel_row = jnp.full((1, 128), -1, jnp.int32)
    for s in range(slots):
        p = jnp.maximum(my_patch[s], 0)
        first_row = (p >> 1) * rows + anchor[0, p]
        first_col = anchor[1, p]
        hit = (
            (grow >= first_row) & (grow < first_row + bl)
            & (gcol >= first_col) & (gcol < first_col + bl) & (my_patch[s] >= 0)
        )
        rel_col = jnp.where(hit, gcol - first_col, rel_col)
        rel_row = jnp.where(hit, grow - first_row + bl * s, rel_row)
    pick_col = jnp.where(rc_i == rel_col, 1.0, 0.0)
    found = dot(mean, pick_col)
    value = value + jnp.sum(
        jnp.where(iota((bl * slots, 128), 0) == rel_row, found, 0.0), axis=0, keepdims=True
    )
    z_s[0] = value

    def send_member(k, carry):
        pltpu.make_async_remote_copy(
            src_ref=z_s.at[0], dst_ref=z_r.at[k], send_sem=send_sem.at[5],
            recv_sem=recv_sem.at[5], device_id=(lax.rem(mem + k + 1, nm), me),
            device_id_type=MESH,
        ).start()
        return carry

    lax.fori_loop(0, nm - 1, send_member, 0)
    all_of(z_r, nm - 1, recv_sem.at[5])

    def weight(m):
        return (1.0 + 2.0 * m.astype(f32) / (nm - 1)) / (2.0 * nm)

    center = weight(mem) * value
    for k in range(nm - 1):
        center = center + weight(lax.rem(mem - k - 1 + nm, nm)) * z_r[k]
    g_s[0] = value - center

    def send_gauge(k, carry):
        pltpu.make_async_remote_copy(
            src_ref=g_s.at[0], dst_ref=g_r.at[k], send_sem=send_sem.at[6],
            recv_sem=recv_sem.at[6], device_id=(mem, lax.rem(me + k + 1, ns)),
            device_id_type=MESH,
        ).start()
        return carry

    lax.fori_loop(0, ns - 1, send_gauge, 0)

    all_of(a2_r, ns - 1, recv_sem.at[4])
    for j in range(2):
        at = owner_at[j]
        tail = jnp.zeros((8, 128), f32)
        for i in range(3):
            piece = a2_r[at, 8 * i : 8 * i + 8, :]
            pz[j, 32 + 8 * i : 40 + 8 * i, :] = piece
            here = (lane8 >= 32 * i) & (lane8 < 32 * i + 32)
            tail = jnp.where(here, roll(piece, 32 + 32 * i, 1), tail)
        pz[j, 56:64, :] = tail
        moved = pz[j, pl.ds(32 - r0[j], rows), :]
        inside = (
            (rowc >= r0[j]) & (rowc < r0[j] + bl) & (lanec >= c0[j]) & (lanec < c0[j] + bl)
        )
        for field in range(3):
            placed = roll(moved, (c0[j] - 32 * field) & 127, 1)
            placed = jnp.concatenate([placed] * (cols // 128), axis=1)
            cout[field] = jnp.where(inside, placed, cout[field])
    final = pltpu.make_async_copy(cout, coarse_out.at[0], out_sem.at[3])
    final.start()

    all_of(g_r, ns - 1, recv_sem.at[6])
    total = g_s[0]
    for k in range(ns - 1):
        total = total + g_r[k]
    spread_out[...] = total

    all_of(pay_r, ns - 1, send_sem.at[2])
    all_of(m1_r, ns - 1, send_sem.at[3])
    all_of(a2_r, ns - 1, send_sem.at[4])
    all_of(z_r, nm - 1, send_sem.at[5])
    all_of(g_r, ns - 1, send_sem.at[6])
    for store in stores:
        store.wait()
    final.wait()


def shards(
    coarse_state, coarse_seabed, open_faces, fine_state, fine_seabed, slot_patch, patch_anchor,
    gauge_cells,
):
    ns = lax.axis_size("space")
    nm = lax.axis_size("member")
    rows, cols = coarse_seabed.shape
    slots, fl = fine_seabed.shape[0], fine_seabed.shape[-1]
    nb = 8 * slots
    vmem, hbm, smem = (
        pl.BlockSpec(memory_space=space) for space in (pltpu.VMEM, pltpu.HBM, pltpu.SMEM)
    )

    def buf(*shape):
        return pltpu.VMEM(shape, f32)

    return pl.pallas_call(
        functools.partial(kernel, ns, nm, slots),
        out_shape=(
            jax.ShapeDtypeStruct(coarse_state.shape, f32),
            jax.ShapeDtypeStruct(fine_state.shape, f32),
            jax.ShapeDtypeStruct((1, gauge_cells.shape[0]), f32),
        ),
        in_specs=[smem, smem, vmem, hbm, hbm, hbm, hbm, hbm],
        out_specs=(hbm, hbm, vmem),
        scratch_shapes=[
            buf(3, rows, cols), buf(rows, cols), pltpu.VMEM((2, rows, cols), jnp.int32),
            buf(3, rows, cols), buf(rows, cols), buf(11, cols // 128, rows, 128),
            buf(rows, cols), buf(rows, cols),
            buf(slots, fl + 16, fl), buf(slots, fl, fl), buf(slots, fl + 16, fl),
            buf(slots, fl, fl),
            buf(8, cols), buf(8, cols), buf(8, cols), buf(8, cols),
            buf(2, 4, 2, 8, 128), buf(8, 128), buf(ns, 8, 128), buf(nb, 128), buf(nb, 128),
            buf(fl, 128), buf(2 * nb, 128), buf(3, slots * fl // REFINE, 128),
            buf(slots, 128, 128),
            buf(slots, 1, 128), buf(ns, 1, 128), buf(ns, 1, 128),
            buf(slots, 24, 128), buf(ns, 24, 128), buf(ns, 24, 128),
            buf(2, 128, 128), buf(3, rows, cols),
            buf(1, 1, 128), buf(nm, 1, 128), buf(1, 1, 128), buf(ns, 1, 128),
            pltpu.SMEM((ns,), jnp.int32),
            pltpu.SemaphoreType.DMA((7,)), pltpu.SemaphoreType.DMA((4,)),
            pltpu.SemaphoreType.DMA((7,)), pltpu.SemaphoreType.DMA((7,)),
        ],
        compiler_params=pltpu.CompilerParams(
            collective_id=0, has_side_effects=True, vmem_limit_bytes=40 * 1024 * 1024
        ),
    )(
        slot_patch, patch_anchor.T, gauge_cells.reshape(1, -1), coarse_state, coarse_seabed,
        open_faces, fine_state, fine_seabed,
    )


def solution(mesh):
    return jax.shard_map(
        shards,
        mesh=mesh,
        in_specs=(
            P("member", None, "space", None),
            P("space", None),
            P(None, "space", None),
            P("member", None, "space", None, None),
            P("space", None, None),
            P(),
            P(),
            P(),
        ),
        out_specs=(
            P("member", None, "space", None),
            P("member", None, "space", None, None),
            P("member", None),
        ),
        check_vma=False,
    )
```

time: 306 us -> 62.1 us (0.20)
  blocking collectives: 107 us -> 0 us
  local copies, waits for them, and re-layouts: 83.4 us -> 9.39 us
  Pallas kernels: 0 us -> 51.7 us
  other arithmetic: 35.9 us -> 0 us
  starting transfers between devices: 33.8 us -> 0 us
  waiting for transfers between devices: 28.6 us -> 0 us
  between operations: 14.5 us -> 0.66 us
    psum x1 -> x0, blocking collectives: 107 us -> none  [shards(): totals = lax.psum(everyone, ('member', 'space'))]
    pallas_call x0 -> x1, Pallas kernels: none -> 51.7 us  [shards(): pl.pallas_call(functools.partial(kernel, ns, nm, slots), out_shape=(jax.S...]
    another operation x4 -> x0, local copies, waits for them, and re-layouts: 28.7 us -> none  [the longest x2 28.7 us: block_average(): height_means = fine_fields[:, 0].reshape(members, slot_count, block_len,...]
    all_to_all x4 -> x0, waiting for transfers between devices: 26 us -> none  [shards(): lax.all_to_all(outgoing, 'space', split_axis=0, concat_axis=0, tiled=True)]
    all_to_all x4 -> x0, starting transfers between devices: 19.2 us -> none  [shards(): lax.all_to_all(outgoing, 'space', split_axis=0, concat_axis=0, tiled=True)]
    concatenate x66 -> x0, local copies, waits for them, and re-layouts: 17.5 us -> none  [the longest x22 7.69 us: fine_advance(): jnp.concatenate([height[..., 1:], east_edge[..., :, None]], axis=-1)]
    ppermute x4 -> x0, starting transfers between devices: 14.6 us -> none  [from_behind(): lax.ppermute(value, axis, [(source, source + steps) for source in range(l...]
    reduce_sum x16 -> x0, other arithmetic: 14 us -> none  [the longest x2 11.2 us: block_average(): height_means = fine_fields[:, 0].reshape(members, slot_count, block_len,...]
  transfers between devices with their start and end apart: 8 -> 0, of which waited for: 6 -> 0; matrix products, arithmetic and copies ran while one was open for 3% -> 0% of each run, Pallas kernels for 0% -> 0%
where the time goes in v1:
time: 62.1 us; the launch traced here: 61.8 us
  Pallas kernels  51.7 us (83%)
  local copies, waits for them, and re-layouts  9.39 us (15%)
  between operations  0.66 us (1%)
    pallas_call x1, Pallas kernels, shards(): pl.pallas_call(functools.partial(kernel, ns, nm, slots), out_shape=(jax.S...  51.7 us
    unnamed x19, local copies, waits for them, and re-layouts  9.39 us

profile of v1, /device:TPU:1, one launch (start us, length us, event | category | flops | bytes accessed | tf_op | source)
XLA Modules:
  0.0 61.8 jit_solution(4992292862935144797)
XLA Ops:
  0.6 0.0 copy-start
  0.6 1.3 %copy-done = f32[1,3,6,128,128]{4,3,2,1,0:T(8,128)S(1)} copy-done((f32[1,3,6,128,128]{4,3,2,1,0:T(8,128)S(1)}, f32[1,3,6,128,128]{4,3,2,1,0:T(8,128)}, u32[]{:S(2)}) %copy-start) | copy-done | bytes 1179672
  1.9 0.0 copy-start.1
  1.9 1.0 %copy-done.1 = f32[1,3,64,512]{3,2,1,0:T(8,128)S(1)} copy-done((f32[1,3,64,512]{3,2,1,0:T(8,128)S(1)}, f32[1,3,64,512]{3,2,1,0:T(8,128)}, u32[]{:S(2)}) %copy-start.1) | copy-done | bytes 393240
  2.9 0.0 copy-start.2
  2.9 1.0 %copy-done.2 = f32[6,128,128]{2,1,0:T(8,128)S(1)} copy-done((f32[6,128,128]{2,1,0:T(8,128)S(1)}, f32[6,128,128]{2,1,0:T(8,128)}, u32[]{:S(2)}) %copy-start.2) | copy-done | bytes 393240
  3.9 0.0 copy-start.3
  3.9 0.9 %copy-done.3 = s32[2,64,512]{2,1,0:T(8,128)S(1)} copy-done((s32[2,64,512]{2,1,0:T(8,128)S(1)}, s32[2,64,512]{2,1,0:T(8,128)}, u32[]{:S(2)}) %copy-start.3) | copy-done | bytes 262168
  4.8 0.0 copy-start.4
  4.8 0.9 %copy-done.4 = f32[64,512]{1,0:T(8,128)S(1)} copy-done((f32[64,512]{1,0:T(8,128)S(1)}, f32[64,512]{1,0:T(8,128)}, u32[]{:S(2)}) %copy-start.4) | copy-done | bytes 131096
  5.8 0.0 copy-start.5
  5.8 0.7 %copy-done.5 = s32[192]{0:T(256)S(1)} copy-done((s32[192]{0:T(256)S(1)}, s32[192]{0:T(256)}, u32[]{:S(2)}) %copy-start.5) | copy-done | bytes 792
  6.4 0.0 copy-start.6
  6.4 0.7 %copy-done.6 = s32[64,2]{0,1:T(2,128)S(1)} copy-done((s32[64,2]{0,1:T(2,128)S(1)}, s32[64,2]{0,1:T(2,128)}, u32[]{:S(2)}) %copy-start.6) | copy-done | bytes 536
  7.1 0.0 copy-start.7
  7.1 0.7 %copy-done.7 = s32[128]{0:T(128)S(1)} copy-done((s32[128]{0:T(128)S(1)}, s32[128]{0:T(128)}, u32[]{:S(2)}) %copy-start.7) | copy-done | bytes 536
  7.8 51.7 %shard_map.103 = (f32[1,3,64,512]{3,2,1,0:T(8,128)S(1)}, f32[1,3,6,128,128]{4,3,2,1,0:T(8,128)S(1)}, f32[1,128]{1,0:T(1,128)S(1)}) custom-call(s32[192]{0:T(256)S(1)} %copy-done.5, s32[2,64]{1,0:T(2,128)S(1)} %bitcast.2, s32[1,128]{1,0:T(1,128)S(1)} %bitcast.3, f32[1,3,64,512]{3,2,1,0:T(8,128)S(1)} %copy-done.1, f32[64,512]{1,0:T(8,128)S(1)} %copy-done.4, ...), custom_call_target="tpu_custom_call" | custom-call | tf_op jit(solution)/shard_map/pallas_call | solution.py:559
  59.5 0.7 %copy.14 = f32[1,3,64,512]{3,2,1,0:T(8,128)} copy(f32[1,3,64,512]{3,2,1,0:T(8,128)S(1)} %get-tuple-element.6) | data formatting | bytes 786432
  60.3 1.0 %copy.15 = f32[1,3,6,128,128]{4,3,2,1,0:T(8,128)} copy(f32[1,3,6,128,128]{4,3,2,1,0:T(8,128)S(1)} %get-tuple-element.7) | data formatting | bytes 2359296
  61.3 0.5 copy.16
Async XLA Ops:
  0.6 1.3 %copy-start = (f32[1,3,6,128,128]{4,3,2,1,0:T(8,128)S(1)}, f32[1,3,6,128,128]{4,3,2,1,0:T(8,128)}, u32[]{:S(2)}) copy-start(f32[1,3,6,128,128]{4,3,2,1,0:T(8,128)} %fine.1) | copy-start | bytes 3538948
  1.9 1.0 %copy-start.1 = (f32[1,3,64,512]{3,2,1,0:T(8,128)S(1)}, f32[1,3,64,512]{3,2,1,0:T(8,128)}, u32[]{:S(2)}) copy-start(f32[1,3,64,512]{3,2,1,0:T(8,128)} %coarse.1) | copy-start | bytes 1179652
  2.9 1.0 %copy-start.2 = (f32[6,128,128]{2,1,0:T(8,128)S(1)}, f32[6,128,128]{2,1,0:T(8,128)}, u32[]{:S(2)}) copy-start(f32[6,128,128]{2,1,0:T(8,128)} %fseabed.1) | copy-start | bytes 1179652
  3.9 0.9 %copy-start.3 = (s32[2,64,512]{2,1,0:T(8,128)S(1)}, s32[2,64,512]{2,1,0:T(8,128)}, u32[]{:S(2)}) copy-start(s32[2,64,512]{2,1,0:T(8,128)} %faces.1) | copy-start | bytes 786436
  4.8 0.9 %copy-start.4 = (f32[64,512]{1,0:T(8,128)S(1)}, f32[64,512]{1,0:T(8,128)}, u32[]{:S(2)}) copy-start(f32[64,512]{1,0:T(8,128)} %seabed.1) | copy-start | bytes 393220
  5.8 0.7 %copy-start.5 = (s32[192]{0:T(256)S(1)}, s32[192]{0:T(256)}, u32[]{:S(2)}) copy-start(s32[192]{0:T(256)} %slot.1) | copy-start | bytes 2308
  6.4 0.7 %copy-start.6 = (s32[64,2]{0,1:T(2,128)S(1)}, s32[64,2]{0,1:T(2,128)}, u32[]{:S(2)}) copy-start(s32[64,2]{0,1:T(2,128)} %param.14) | copy-start | bytes 1540
  7.1 0.7 %copy-start.7 = (s32[128]{0:T(128)S(1)}, s32[128]{0:T(128)}, u32[]{:S(2)}) copy-start(s32[128]{0:T(128)} %param.15) | copy-start | bytes 1540

commit v2 on v1

--- a/solution.py
+++ b/solution.py
@@ -21,6 +21,17 @@
     )
 
 
+def dot3(a, b):
+    b = b.astype(jnp.bfloat16)
+    total = None
+    for _ in range(3):
+        part = a.astype(jnp.bfloat16)
+        a = a - part.astype(f32)
+        term = lax.dot_general(part, b, NN, preferred_element_type=f32)
+        total = term if total is None else total + term
+    return total
+
+
 def iota(shape, dim):
     return lax.broadcasted_iota(jnp.int32, shape, dim)
 
@@ -33,10 +44,10 @@
     ns, nm, slots,
     slot, anchor, gauge, coarse, seabed, faces, fine, fseabed,
     coarse_out, fine_out, spread_out,
-    cs, sd, op, t1, t2, ex, ce, cn, fh, fu, fv, fd,
+    cs, sd, op, t1, t2, ex, ce, cn, fh, fu, fv, fd, eo, ed,
     up_s, dn_s, up_r, dn_r, rs, pay_s, pay_r, xb, gx, ycol, yrow, red, tp,
-    m1_p, m1_s, m1_r, a2_p, a2_s, a2_r, pz, cout, z_s, z_r, g_s, g_r, sidx,
-    in_sem, out_sem, send_sem, recv_sem,
+    m1_p, m1_s, m1_r, a2_p, a2_s, a2_r, pz, z_s, z_r, g_s, g_r, sidx,
+    in_sem, send_sem, recv_sem,
 ):
     me = lax.axis_index("space")
     mem = lax.axis_index("member")
@@ -44,6 +55,23 @@
     fl = fu.shape[-1]
     bl = fl // REFINE
     nb = slots * 8
+
+    barrier = pltpu.get_barrier_semaphore()
+
+    def greet_space(k, carry):
+        pl.semaphore_signal(
+            barrier, inc=1, device_id=(mem, lax.rem(me + k, ns)), device_id_type=MESH
+        )
+        return carry
+
+    def greet_member(k, carry):
+        pl.semaphore_signal(
+            barrier, inc=1, device_id=(lax.rem(mem + k, nm), me), device_id_type=MESH
+        )
+        return carry
+
+    lax.fori_loop(1, nm, greet_member, 0)
+    lax.fori_loop(1, ns, greet_space, 0)
 
     loads = [
         pltpu.make_async_copy(coarse.at[0], cs, in_sem.at[0]),
@@ -57,44 +85,6 @@
     for load in loads:
         load.start()
 
-    barrier = pltpu.get_barrier_semaphore()
-
-    def greet_space(k, carry):
-        pl.semaphore_signal(
-            barrier, inc=1, device_id=(mem, lax.rem(me + k, ns)), device_id_type=MESH
-        )
-        return carry
-
-    def greet_member(k, carry):
-        pl.semaphore_signal(
-            barrier, inc=1, device_id=(lax.rem(mem + k, nm), me), device_id_type=MESH
-        )
-        return carry
-
-    lax.fori_loop(1, ns, greet_space, 0)
-    lax.fori_loop(1, nm, greet_member, 0)
-
-    my_patch = [slot[me * slots + s] for s in range(slots)]
-    held_parent = [p >> 1 for p in my_patch]
-
-    def find_slot(k, carry):
-        d = lax.rem(me + k + 1, ns)
-        which = jnp.int32(0)
-        for s in range(1, slots):
-            which = jnp.where(held_parent[s] == d, s, which)
-        sidx[k] = which
-        return carry
-
-    lax.fori_loop(0, ns, find_slot, 0)
-
-    def find_owner(i, carry):
-        p = slot[i]
-        return tuple(
-            jnp.where(p == 2 * me + j, i, carry[j]) for j in range(2)
-        )
-
-    where_held = lax.fori_loop(0, ns * slots, find_owner, (jnp.int32(0), jnp.int32(0)))
-    owner_at = [lax.rem(me - w // slots - 1 + 2 * ns, ns) for w in where_held]
     r0 = [jnp.clip(anchor[0, 2 * me + j], 1, rows - bl - 1) for j in range(2)]
     c0 = [jnp.clip(anchor[1, 2 * me + j], 1, cols - bl - 1) for j in range(2)]
 
@@ -248,6 +238,28 @@
 
     lax.fori_loop(0, ns - 1, spread_payload, 0)
 
+    my_patch = [slot[me * slots + s] for s in range(slots)]
+    held_parent = [p >> 1 for p in my_patch]
+
+    def find_slot(k, carry):
+        d = lax.rem(me + k + 1, ns)
+        which = jnp.int32(0)
+        for s in range(1, slots):
+            which = jnp.where(held_parent[s] == d, s, which)
+        sidx[k] = which
+        return carry
+
+    lax.fori_loop(0, ns, find_slot, 0)
+
+    def find_owner(i, carry):
+        p = slot[i]
+        return tuple(
+            jnp.where(p == 2 * me + j, i, carry[j]) for j in range(2)
+        )
+
+    where_held = lax.fori_loop(0, ns * slots, find_owner, (jnp.int32(0), jnp.int32(0)))
+    owner_at = [lax.rem(me - w // slots - 1 + 2 * ns, ns) for w in where_held]
+
     def all_of(ref, count, sem):
         part = ref.at[pl.ds(0, count)]
         pltpu.make_async_copy(part, part, sem).wait()
@@ -265,54 +277,75 @@
         both = jnp.concatenate([old, diff], axis=0)
         ycol[:, 0 : 2 * nb] = dot(spread_rows, both, NT)
         yrow[...] = dot(both, spread_lanes)
-
-    def fine_steps(last):
-        lane_f = iota((fl, 128), 1)
-
-        def one_slot(s, carry):
-            ego = roll(ycol[...], 127 - 8 * s, 1)
-            egd = roll(ycol[...], lax.rem(255 - 8 * s - nb, 128), 1)
-            n_old = yrow[pl.ds(8 * s + 2, 1), :]
-            s_old = yrow[pl.ds(8 * s + 3, 1), :]
-            n_dif = yrow[pl.ds(nb + 8 * s + 2, 1), :]
-            s_dif = yrow[pl.ds(nb + 8 * s + 3, 1), :]
+        for s in range(slots):
+            eo[s] = roll(ycol[...], 127 - 8 * s, 1)
+            ed[s] = roll(ycol[...], (255 - 8 * s - nb) % 128, 1)
+
+    lane_f = iota((fl, 128), 1)
+    every = range(slots)
+
+    def update(k, final):
+        kf = k.astype(f32)
+        wf = (2.0 * kf + 1.0) / (2.0 * REFINE)
+        wl = (kf + 1.0) / REFINE
+        weight_of = jnp.where(lane == fl - 1, wl, wf)
+        for s in every:
+            n, o = 8 * s + 2, 8 * s + 3
+            fv[s, 7:8, :] = yrow[o : o + 1, :] + wf * yrow[nb + o : nb + o + 1, :]
+            fh[s, 8 + fl : 9 + fl, :] = yrow[n : n + 1, :] + wl * yrow[nb + n : nb + n + 1, :]
+        held = []
+        for s in every:
+            edge = eo[s] + weight_of * ed[s]
+            u = fu[s]
+            v = fv[s, 8 : 8 + fl, :]
+            v_s = fv[s, 7 : 7 + fl, :]
+            u_w = jnp.where(lane_f == 0, edge, roll(u, 1, 1))
+            h = fh[s, 8 : 8 + fl, :] - C * (u - u_w + v - v_s)
+            held.append((h, u, v, edge))
+        for s in every:
+            fh[s, 8 : 8 + fl, :] = held[s][0]
+        for s in every:
+            h, u, v, edge = held[s]
             cdf = C * fd[s]
-            used = slot[me * slots + s] >= 0
-            for k in range(REFINE):
-                wf = (2 * k + 1) / (2.0 * REFINE)
-                wl = (k + 1) / float(REFINE)
-                edge = ego + jnp.where(lane == fl - 1, wl, wf) * egd
-                u = fu[s]
-                fv[s, 7:8, :] = s_old + wf * s_dif
-                v = fv[s, 8 : 8 + fl, :]
-                v_s = fv[s, 7 : 7 + fl, :]
-                u_w = jnp.where(lane_f == 0, edge, roll(u, 1, 1))
-                h = fh[s, 8 : 8 + fl, :] - C * (u - u_w + v - v_s)
-                fh[s, 8 : 8 + fl, :] = h
-                fh[s, 8 + fl : 9 + fl, :] = n_old + wl * n_dif
-                h_e = jnp.where(lane_f == fl - 1, edge, roll(h, fl - 1, 1))
-                h_n = fh[s, 9 : 9 + fl, :]
-                u = u - cdf * (h_e - h)
-                v = v - cdf * (h_n - h)
-                if last and k == REFINE - 1:
-                    fh[s, 8 : 8 + fl, :] = jnp.where(used, h, 0.0)
-                    u = jnp.where(used, u, 0.0)
-                    v = jnp.where(used, v, 0.0)
+            h_e = jnp.where(lane_f == fl - 1, edge, roll(h, fl - 1, 1))
+            h_n = fh[s, 9 : 9 + fl, :]
+            u = u - cdf * (h_e - h)
+            v = v - cdf * (h_n - h)
+            if final:
+                used = my_patch[s] >= 0
+                fine_out[0, 0, s] = jnp.where(used, h, 0.0)
+                fine_out[0, 1, s] = jnp.where(used, u, 0.0)
+                fine_out[0, 2, s] = jnp.where(used, v, 0.0)
+            else:
                 fu[s] = u
                 fv[s, 8 : 8 + fl, :] = v
+
+    def fine_steps(last):
+        def step(k, carry):
+            update(k, False)
             return carry
 
-        lax.fori_loop(0, slots, one_slot, 0)
-
-    def averages():
+        lax.fori_loop(0, REFINE - 1 if last else REFINE, step, 0)
+        if last:
+            update(jnp.int32(REFINE - 1), True)
+
+    def averages(held):
         for s in range(slots):
             span = slice(bl * s, bl * s + bl)
-            parts = [fh[s, pl.ds(8 + i, bl, stride=4), :] for i in range(REFINE)]
+            parts = [held(0, s, i) for i in range(REFINE)]
             red[0, span, :] = 0.25 * ((parts[0] + parts[1]) + (parts[2] + parts[3]))
-            parts = [fu[s, pl.ds(i, bl, stride=4), :] for i in range(REFINE)]
+            parts = [held(1, s, i) for i in range(REFINE)]
             red[1, span, :] = 0.25 * ((parts[0] + parts[1]) + (parts[2] + parts[3]))
-            red[2, span, :] = fv[s, pl.ds(11, bl, stride=4), :]
-        return dot(red[0], mean_h) + dot(red[1], mean_u) + dot(red[2], mean_v)
+            red[2, span, :] = held(2, s, REFINE - 1)
+        return dot3(red[0], mean_h) + dot3(red[1], mean_u) + dot3(red[2], mean_v)
+
+    def inner(f, s, i):
+        if f == 1:
+            return fu[s, pl.ds(i, bl, stride=REFINE), :]
+        return (fh, None, fv)[f][s, pl.ds(8 + i, bl, stride=REFINE), :]
+
+    def outer(f, s, i):
+        return fine_out[0, f, s, pl.ds(i, bl, stride=REFINE), :]
 
     for load in loads[3:]:
         load.wait()
@@ -331,7 +364,7 @@
     )
     fine_steps(False)
 
-    mean = averages()
+    mean = averages(inner)
     pick_i = iota((16, 128), 0)
     pick_l = iota((16, 128), 1)
     pick = jnp.where((pick_i == 0) & (pick_l == 63), C, 0.0)
@@ -377,34 +410,7 @@
     m1_r[ns - 1] = m1_p[sidx[ns - 1]]
 
     fine_steps(True)
-    stores = [
-        pltpu.make_async_copy(fh.at[:, pl.ds(8, fl), :], fine_out.at[0, 0], out_sem.at[0]),
-        pltpu.make_async_copy(fu, fine_out.at[0, 1], out_sem.at[1]),
-        pltpu.make_async_copy(fv.at[:, pl.ds(8, fl), :], fine_out.at[0, 2], out_sem.at[2]),
-    ]
-
-    mean = averages()
-    for s in range(slots):
-        tail = mean[bl * s + 24 : bl * s + 32]
-        for i in range(3):
-            piece = mean[bl * s + 8 * i : bl * s + 8 * i + 8]
-            a2_p[s, 8 * i : 8 * i + 8, :] = jnp.where(
-                lane8 < 96, piece, roll(tail, 96 - 32 * i, 1)
-            )
-
-    def send_mean(k, carry):
-        a2_s[k] = a2_p[sidx[k]]
-        pltpu.make_async_remote_copy(
-            src_ref=a2_s.at[k], dst_ref=a2_r.at[k], send_sem=send_sem.at[4],
-            recv_sem=recv_sem.at[4], device_id=(mem, lax.rem(me + k + 1, ns)),
-            device_id_type=MESH,
-        ).start()
-        return carry
-
-    lax.fori_loop(0, ns - 1, send_mean, 0)
-    a2_r[ns - 1] = a2_p[sidx[ns - 1]]
-    for store in stores:
-        store.start()
+    mean = averages(outer)
 
     all_of(m1_r, ns - 1, recv_sem.at[3])
     rowh = iota((rows, 128), 0)
@@ -437,7 +443,7 @@
     for at_west, west_col, at_south, south_row in fixes:
         u2 = jnp.where(at_west, west_col, u2)
         v2 = jnp.where(at_south, south_row, v2)
-    cout[0], cout[1], cout[2] = h2, u2, v2
+    coarse_out[0, 0], coarse_out[0, 1], coarse_out[0, 2] = h2, u2, v2
 
     cell = gauge[...]
     grow = cell // cols
@@ -483,6 +489,26 @@
         return carry
 
     lax.fori_loop(0, nm - 1, send_member, 0)
+    for s in range(slots):
+        tail = mean[bl * s + 24 : bl * s + 32]
+        for i in range(3):
+            piece = mean[bl * s + 8 * i : bl * s + 8 * i + 8]
+            a2_p[s, 8 * i : 8 * i + 8, :] = jnp.where(
+                lane8 < 96, piece, roll(tail, 96 - 32 * i, 1)
+            )
+
+    def send_mean(k, carry):
+        a2_s[k] = a2_p[sidx[k]]
+        pltpu.make_async_remote_copy(
+            src_ref=a2_s.at[k], dst_ref=a2_r.at[k], send_sem=send_sem.at[4],
+            recv_sem=recv_sem.at[4], device_id=(mem, lax.rem(me + k + 1, ns)),
+            device_id_type=MESH,
+        ).start()
+        return carry
+
+    lax.fori_loop(0, ns - 1, send_mean, 0)
+    a2_r[ns - 1] = a2_p[sidx[ns - 1]]
+
     all_of(z_r, nm - 1, recv_sem.at[5])
 
     def weight(m):
@@ -520,9 +546,7 @@
         for field in range(3):
             placed = roll(moved, (c0[j] - 32 * field) & 127, 1)
             placed = jnp.concatenate([placed] * (cols // 128), axis=1)
-            cout[field] = jnp.where(inside, placed, cout[field])
-    final = pltpu.make_async_copy(cout, coarse_out.at[0], out_sem.at[3])
-    final.start()
+            coarse_out[0, field] = jnp.where(inside, placed, coarse_out[0, field])
 
     all_of(g_r, ns - 1, recv_sem.at[6])
     total = g_s[0]
@@ -535,9 +559,15 @@
     all_of(a2_r, ns - 1, send_sem.at[4])
     all_of(z_r, nm - 1, send_sem.at[5])
     all_of(g_r, ns - 1, send_sem.at[6])
-    for store in stores:
-        store.wait()
-    final.wait()
+
+
+def store_results(coarse, fine, spread, coarse_out, fine_out, spread_out, sem):
+    pairs = ((coarse, coarse_out), (fine, fine_out), (spread, spread_out))
+    copies = [pltpu.make_async_copy(a, b, sem.at[i]) for i, (a, b) in enumerate(pairs)]
+    for copy in copies:
+        copy.start()
+    for copy in copies:
+        copy.wait()
 
 
 def shards(
@@ -556,40 +586,45 @@
     def buf(*shape):
         return pltpu.VMEM(shape, f32)
 
-    return pl.pallas_call(
+    shapes = (coarse_state.shape, fine_state.shape, (1, gauge_cells.shape[0]))
+    results = pl.pallas_call(
         functools.partial(kernel, ns, nm, slots),
-        out_shape=(
-            jax.ShapeDtypeStruct(coarse_state.shape, f32),
-            jax.ShapeDtypeStruct(fine_state.shape, f32),
-            jax.ShapeDtypeStruct((1, gauge_cells.shape[0]), f32),
-        ),
+        out_shape=tuple(pltpu.VMEM(shape, f32) for shape in shapes),
         in_specs=[smem, smem, vmem, hbm, hbm, hbm, hbm, hbm],
-        out_specs=(hbm, hbm, vmem),
+        out_specs=(vmem, vmem, vmem),
         scratch_shapes=[
             buf(3, rows, cols), buf(rows, cols), pltpu.VMEM((2, rows, cols), jnp.int32),
             buf(3, rows, cols), buf(rows, cols), buf(11, cols // 128, rows, 128),
             buf(rows, cols), buf(rows, cols),
             buf(slots, fl + 16, fl), buf(slots, fl, fl), buf(slots, fl + 16, fl),
-            buf(slots, fl, fl),
+            buf(slots, fl, fl), buf(slots, fl, 128), buf(slots, fl, 128),
             buf(8, cols), buf(8, cols), buf(8, cols), buf(8, cols),
             buf(2, 4, 2, 8, 128), buf(8, 128), buf(ns, 8, 128), buf(nb, 128), buf(nb, 128),
             buf(fl, 128), buf(2 * nb, 128), buf(3, slots * fl // REFINE, 128),
             buf(slots, 128, 128),
             buf(slots, 1, 128), buf(ns, 1, 128), buf(ns, 1, 128),
             buf(slots, 24, 128), buf(ns, 24, 128), buf(ns, 24, 128),
-            buf(2, 128, 128), buf(3, rows, cols),
+            buf(2, 128, 128),
             buf(1, 1, 128), buf(nm, 1, 128), buf(1, 1, 128), buf(ns, 1, 128),
             pltpu.SMEM((ns,), jnp.int32),
-            pltpu.SemaphoreType.DMA((7,)), pltpu.SemaphoreType.DMA((4,)),
             pltpu.SemaphoreType.DMA((7,)), pltpu.SemaphoreType.DMA((7,)),
+            pltpu.SemaphoreType.DMA((7,)),
         ],
         compiler_params=pltpu.CompilerParams(
-            collective_id=0, has_side_effects=True, vmem_limit_bytes=40 * 1024 * 1024
+            collective_id=0, has_side_effects=True, vmem_limit_bytes=56 * 1024 * 1024
         ),
     )(
-        slot_patch, patch_anchor.T, gauge_cells.reshape(1, -1), coarse_state, coarse_seabed,
-        open_faces, fine_state, fine_seabed,
-    )
+        slot_patch, patch_anchor.T, gauge_cells.reshape(1, -1),
+        *(pltpu.with_memory_space_constraint(x, pltpu.HBM)
+          for x in (coarse_state, coarse_seabed, open_faces, fine_state, fine_seabed)),
+    )
+    return pl.pallas_call(
+        store_results,
+        out_shape=tuple(jax.ShapeDtypeStruct(shape, f32) for shape in shapes),
+        in_specs=[vmem] * 3,
+        out_specs=(hbm,) * 3,
+        scratch_shapes=[pltpu.SemaphoreType.DMA((3,))],
+    )(*(pltpu.with_memory_space_constraint(x, pltpu.VMEM) for x in results))
 
 
 def solution(mesh):

time: 62.1 us -> 48.4 us (0.78)
  local copies, waits for them, and re-layouts: 9.39 us -> 0 us
  Pallas kernels: 51.7 us -> 47.6 us
    unnamed x19 -> x0, local copies, waits for them, and re-layouts: 9.39 us -> none
    pallas_call x1 -> x2, Pallas kernels: 51.7 us -> 47.6 us  [the longest x1 46.4 us: shards(): pl.pallas_call(functools.partial(kernel, ns, nm, slots), out_shape=tuple(...]
where the time goes in v2:
time: 48.4 us; the launch traced here: 48.2 us
  Pallas kernels  47.6 us (98%)
  between operations  0.64 us (1%)
    pallas_call x1, Pallas kernels, shards(): pl.pallas_call(functools.partial(kernel, ns, nm, slots), out_shape=tuple(...  46.4 us
    pallas_call x1, Pallas kernels, shards(): pl.pallas_call(store_results, out_shape=tuple((jax.ShapeDtypeStruct(shape...  1.17 us

profile of v2, /device:TPU:1, one launch (start us, length us, event | category | flops | bytes accessed | tf_op | source)
XLA Modules:
  0.0 48.2 jit_solution(1332772386435868143)
XLA Ops:
  0.6 46.4 %shard_map.103 = (f32[1,3,64,512]{3,2,1,0:T(8,128)S(1)}, f32[1,3,6,128,128]{4,3,2,1,0:T(8,128)S(1)}, f32[1,128]{1,0:T(1,128)S(1)}) custom-call(s32[192]{0:T(256)} %slot.1, s32[2,64]{1,0:T(2,128)} %bitcast.2, s32[1,128]{1,0:T(1,128)} %bitcast.3, f32[1,3,64,512]{3,2,1,0:T(8,128)} %coarse.1, f32[64,512]{1,0:T(8,128)} %seabed.1, s32[2,64,512]{2,1,0:T(8,128)} %faces.1, ...), custom_call_target="tpu_custom_call" | custom-call | tf_op jit(solution)/shard_map/pallas_call | solution.py:590
  47.1 1.2 %shard_map.104 = (f32[1,3,64,512]{3,2,1,0:T(8,128)}, f32[1,3,6,128,128]{4,3,2,1,0:T(8,128)}, f32[1,128]{1,0:T(1,128)}) custom-call(f32[1,3,64,512]{3,2,1,0:T(8,128)S(1)} %get-tuple-element.6.coarse, f32[1,3,6,128,128]{4,3,2,1,0:T(8,128)S(1)} %get-tuple-element.7.fine, f32[1,128]{1,0:T(1,128)S(1)} %get-tuple-element.8.spread), custom_call_target="tpu_custom_call" | custom-call | tf_op jit(solution)/shard_map/pallas_call | solution.py:621

commit v3 on v2

--- a/solution.py
+++ b/solution.py
@@ -263,6 +263,26 @@
     def all_of(ref, count, sem):
         part = ref.at[pl.ds(0, count)]
         pltpu.make_async_copy(part, part, sem).wait()
+
+    cell = gauge[...]
+    grow = cell // cols
+    gcol = cell - grow * cols
+    own_row = grow - me * rows
+    covered = None
+    for j in range(2):
+        down = own_row - r0[j]
+        right = gcol - c0[j]
+        hit = (
+            (down >= 0) & (right >= 0) & (down <= bl) & (right <= bl)
+            & ((down < bl) | (right < bl))
+        )
+        covered = hit if covered is None else covered | hit
+    pick_col = jnp.where(iota((cols, 128), 0) == gcol, 1.0, 0.0)
+    found = dot3(h2, pick_col)
+    outside = jnp.sum(
+        jnp.where((iota((rows, 128), 0) == own_row) & jnp.logical_not(covered), found, 0.0),
+        axis=0, keepdims=True,
+    )
 
     rc_i = iota((fl, 128), 0)
     rc_l = iota((fl, 128), 1)
@@ -389,6 +409,61 @@
         jnp.where((lane_nb >= 32) & (lane_nb < 64), x, 0.0),
         jnp.where(mid, new - roll(x, 32, 1), 0.0),
     )
+    fine_steps(True)
+    mean = averages(outer)
+
+    rel_col = jnp.full((1, 128), -1, jnp.int32)
+    rel_row = jnp.full((1, 128), -1, jnp.int32)
+    for s in range(slots):
+        p = jnp.maximum(my_patch[s], 0)
+        down = jnp.where(my_patch[s] >= 0, grow - ((p >> 1) * rows + anchor[0, p]), -1)
+        right = gcol - anchor[1, p]
+        in_rows = (down >= 0) & (down < bl)
+        in_cols = (right >= 0) & (right < bl)
+        hit = in_rows & in_cols
+        rel_col = jnp.where(hit, right, rel_col)
+        rel_row = jnp.where(hit, down + bl * s, rel_row)
+        hit = in_rows & (right == bl)
+        rel_col = jnp.where(hit, 64 + down, rel_col)
+        rel_row = jnp.where(hit, bl * slots + 8 * s, rel_row)
+        hit = (down == bl) & in_cols
+        rel_col = jnp.where(hit, 64 + right, rel_col)
+        rel_row = jnp.where(hit, bl * slots + 8 * s + 2, rel_row)
+    pick_col = jnp.where(rc_i == rel_col, 1.0, 0.0)
+    found = dot3(jnp.concatenate([mean, new], axis=0), pick_col)
+    at_row = iota((bl * slots + nb, 128), 0) == rel_row
+    value = outside + jnp.sum(jnp.where(at_row, found, 0.0), axis=0, keepdims=True)
+    z_s[0] = value
+
+    def send_member(k, carry):
+        pltpu.make_async_remote_copy(
+            src_ref=z_s.at[0], dst_ref=z_r.at[k], send_sem=send_sem.at[5],
+            recv_sem=recv_sem.at[5], device_id=(lax.rem(mem + k + 1, nm), me),
+            device_id_type=MESH,
+        ).start()
+        return carry
+
+    lax.fori_loop(0, nm - 1, send_member, 0)
+    for s in range(slots):
+        tail = mean[bl * s + 24 : bl * s + 32]
+        for i in range(3):
+            piece = mean[bl * s + 8 * i : bl * s + 8 * i + 8]
+            a2_p[s, 8 * i : 8 * i + 8, :] = jnp.where(
+                lane8 < 96, piece, roll(tail, 96 - 32 * i, 1)
+            )
+
+    def send_mean(k, carry):
+        a2_s[k] = a2_p[sidx[k]]
+        pltpu.make_async_remote_copy(
+            src_ref=a2_s.at[k], dst_ref=a2_r.at[k], send_sem=send_sem.at[4],
+            recv_sem=recv_sem.at[4], device_id=(mem, lax.rem(me + k + 1, ns)),
+            device_id_type=MESH,
+        ).start()
+        return carry
+
+    lax.fori_loop(0, ns - 1, send_mean, 0)
+    a2_r[ns - 1] = a2_p[sidx[ns - 1]]
+
     packed = jnp.zeros((nb, 128), f32)
     row_nb = iota((nb, 128), 0) & 7
     for q in range(4):
@@ -409,8 +484,25 @@
     lax.fori_loop(0, ns - 1, send_cycle, 0)
     m1_r[ns - 1] = m1_p[sidx[ns - 1]]
 
-    fine_steps(True)
-    mean = averages(outer)
+    all_of(z_r, nm - 1, recv_sem.at[5])
+
+    def weight(m):
+        return (1.0 + 2.0 * m.astype(f32) / (nm - 1)) / (2.0 * nm)
+
+    center = weight(mem) * value
+    for k in range(nm - 1):
+        center = center + weight(lax.rem(mem - k - 1 + nm, nm)) * z_r[k]
+    g_s[0] = value - center
+
+    def send_gauge(k, carry):
+        pltpu.make_async_remote_copy(
+            src_ref=g_s.at[0], dst_ref=g_r.at[k], send_sem=send_sem.at[6],
+            recv_sem=recv_sem.at[6], device_id=(mem, lax.rem(me + k + 1, ns)),
+            device_id_type=MESH,
+        ).start()
+        return carry
+
+    lax.fori_loop(0, ns - 1, send_gauge, 0)
 
     all_of(m1_r, ns - 1, recv_sem.at[3])
     rowh = iota((rows, 128), 0)
@@ -444,90 +536,6 @@
         u2 = jnp.where(at_west, west_col, u2)
         v2 = jnp.where(at_south, south_row, v2)
     coarse_out[0, 0], coarse_out[0, 1], coarse_out[0, 2] = h2, u2, v2
-
-    cell = gauge[...]
-    grow = cell // cols
-    gcol = cell - grow * cols
-    own_row = grow - me * rows
-    in_block = None
-    for j in range(2):
-        hit = (
-            (own_row >= r0[j]) & (own_row < r0[j] + bl) & (gcol >= c0[j]) & (gcol < c0[j] + bl)
-        )
-        in_block = hit if in_block is None else in_block | hit
-    pick_col = jnp.where(iota((cols, 128), 0) == gcol, 1.0, 0.0)
-    found = dot(h2, pick_col)
-    value = jnp.sum(
-        jnp.where((rowh == own_row) & jnp.logical_not(in_block), found, 0.0),
-        axis=0, keepdims=True,
-    )
-    rel_col = jnp.full((1, 128), -1, jnp.int32)
-    rel_row = jnp.full((1, 128), -1, jnp.int32)
-    for s in range(slots):
-        p = jnp.maximum(my_patch[s], 0)
-        first_row = (p >> 1) * rows + anchor[0, p]
-        first_col = anchor[1, p]
-        hit = (
-            (grow >= first_row) & (grow < first_row + bl)
-            & (gcol >= first_col) & (gcol < first_col + bl) & (my_patch[s] >= 0)
-        )
-        rel_col = jnp.where(hit, gcol - first_col, rel_col)
-        rel_row = jnp.where(hit, grow - first_row + bl * s, rel_row)
-    pick_col = jnp.where(rc_i == rel_col, 1.0, 0.0)
-    found = dot(mean, pick_col)
-    value = value + jnp.sum(
-        jnp.where(iota((bl * slots, 128), 0) == rel_row, found, 0.0), axis=0, keepdims=True
-    )
-    z_s[0] = value
-
-    def send_member(k, carry):
-        pltpu.make_async_remote_copy(
-            src_ref=z_s.at[0], dst_ref=z_r.at[k], send_sem=send_sem.at[5],
-            recv_sem=recv_sem.at[5], device_id=(lax.rem(mem + k + 1, nm), me),
-            device_id_type=MESH,
-        ).start()
-        return carry
-
-    lax.fori_loop(0, nm - 1, send_member, 0)
-    for s in range(slots):
-        tail = mean[bl * s + 24 : bl * s + 32]
-        for i in range(3):
-            piece = mean[bl * s + 8 * i : bl * s + 8 * i + 8]
-            a2_p[s, 8 * i : 8 * i + 8, :] = jnp.where(
-                lane8 < 96, piece, roll(tail, 96 - 32 * i, 1)
-            )
-
-    def send_mean(k, carry):
-        a2_s[k] = a2_p[sidx[k]]
-        pltpu.make_async_remote_copy(
-            src_ref=a2_s.at[k], dst_ref=a2_r.at[k], send_sem=send_sem.at[4],
-            recv_sem=recv_sem.at[4], device_id=(mem, lax.rem(me + k + 1, ns)),
-            device_id_type=MESH,
-        ).start()
-        return carry
-
-    lax.fori_loop(0, ns - 1, send_mean, 0)
-    a2_r[ns - 1] = a2_p[sidx[ns - 1]]
-
-    all_of(z_r, nm - 1, recv_sem.at[5])
-
-    def weight(m):
-        return (1.0 + 2.0 * m.astype(f32) / (nm - 1)) / (2.0 * nm)
-
-    center = weight(mem) * value
-    for k in range(nm - 1):
-        center = center + weight(lax.rem(mem - k - 1 + nm, nm)) * z_r[k]
-    g_s[0] = value - center
-
-    def send_gauge(k, carry):
-        pltpu.make_async_remote_copy(
-            src_ref=g_s.at[0], dst_ref=g_r.at[k], send_sem=send_sem.at[6],
-            recv_sem=recv_sem.at[6], device_id=(mem, lax.rem(me + k + 1, ns)),
-            device_id_type=MESH,
-        ).start()
-        return carry
-
-    lax.fori_loop(0, ns - 1, send_gauge, 0)
 
     all_of(a2_r, ns - 1, recv_sem.at[4])
     for j in range(2):

time: 48.4 us -> 45.7 us (0.944)
  Pallas kernels: 47.6 us -> 44.9 us
    pallas_call x1, Pallas kernels: 46.4 us -> 43.8 us  [shards(): pl.pallas_call(functools.partial(kernel, ns, nm, slots), out_shape=tuple(...]
where the time goes in v3:
time: 45.7 us; the launch traced here: 45.6 us
  Pallas kernels  44.9 us (98%)
  between operations  0.64 us (1%)
    pallas_call x1, Pallas kernels, shards(): pl.pallas_call(functools.partial(kernel, ns, nm, slots), out_shape=tuple(...  43.8 us
    pallas_call x1, Pallas kernels, shards(): pl.pallas_call(store_results, out_shape=tuple((jax.ShapeDtypeStruct(shape...  1.17 us

profile of v3, /device:TPU:1, one launch (start us, length us, event | category | flops | bytes accessed | tf_op | source)
XLA Modules:
  0.0 45.6 jit_solution(1843218333037361319)
XLA Ops:
  0.6 43.8 %shard_map.103 = (f32[1,3,64,512]{3,2,1,0:T(8,128)S(1)}, f32[1,3,6,128,128]{4,3,2,1,0:T(8,128)S(1)}, f32[1,128]{1,0:T(1,128)S(1)}) custom-call(s32[192]{0:T(256)} %slot.1, s32[2,64]{1,0:T(2,128)} %bitcast.2, s32[1,128]{1,0:T(1,128)} %bitcast.3, f32[1,3,64,512]{3,2,1,0:T(8,128)} %coarse.1, f32[64,512]{1,0:T(8,128)} %seabed.1, s32[2,64,512]{2,1,0:T(8,128)} %faces.1, ...), custom_call_target="tpu_custom_call" | custom-call | tf_op jit(solution)/shard_map/pallas_call | solution.py:598
  44.4 1.2 %shard_map.104 = (f32[1,3,64,512]{3,2,1,0:T(8,128)}, f32[1,3,6,128,128]{4,3,2,1,0:T(8,128)}, f32[1,128]{1,0:T(1,128)}) custom-call(f32[1,3,64,512]{3,2,1,0:T(8,128)S(1)} %get-tuple-element.6.coarse, f32[1,3,6,128,128]{4,3,2,1,0:T(8,128)S(1)} %get-tuple-element.7.fine, f32[1,128]{1,0:T(1,128)S(1)} %get-tuple-element.8.spread), custom_call_target="tpu_custom_call" | custom-call | tf_op jit(solution)/shard_map/pallas_call | solution.py:629

commit v4 on v3

--- a/solution.py
+++ b/solution.py
@@ -21,15 +21,28 @@
     )
 
 
+def terms(x):
+    parts = []
+    for _ in range(3):
+        parts.append(x.astype(jnp.bfloat16))
+        x = x - parts[-1].astype(f32)
+    return parts
+
+
 def dot3(a, b):
     b = b.astype(jnp.bfloat16)
-    total = None
-    for _ in range(3):
-        part = a.astype(jnp.bfloat16)
-        a = a - part.astype(f32)
-        term = lax.dot_general(part, b, NN, preferred_element_type=f32)
-        total = term if total is None else total + term
-    return total
+    one, two, three = (
+        lax.dot_general(part, b, NN, preferred_element_type=f32) for part in terms(a)
+    )
+    return one + (two + three)
+
+
+def dot3_nt(a, b):
+    a = a.astype(jnp.bfloat16)
+    one, two, three = (
+        lax.dot_general(a, part, NT, preferred_element_type=f32) for part in terms(b)
+    )
+    return one + (two + three)
 
 
 def iota(shape, dim):
@@ -45,7 +58,7 @@
     slot, anchor, gauge, coarse, seabed, faces, fine, fseabed,
     coarse_out, fine_out, spread_out,
     cs, sd, op, t1, t2, ex, ce, cn, fh, fu, fv, fd, eo, ed,
-    up_s, dn_s, up_r, dn_r, rs, pay_s, pay_r, xb, gx, ycol, yrow, red, tp,
+    up_s, dn_s, up_r, dn_r, rs, early_s, early_r, pay_s, pay_r, xb, gx, ycol, yrow, red, tp,
     m1_p, m1_s, m1_r, a2_p, a2_s, a2_r, pz, z_s, z_r, g_s, g_r, sidx,
     in_sem, send_sem, recv_sem,
 ):
@@ -58,20 +71,25 @@
 
     barrier = pltpu.get_barrier_semaphore()
 
-    def greet_space(k, carry):
+    def far_first(i):
+        return lax.rem(i + (5 * ns) // 8 - 1, ns - 1)
+
+    def greet_space(i, carry):
+        k = far_first(i) + 1
         pl.semaphore_signal(
             barrier, inc=1, device_id=(mem, lax.rem(me + k, ns)), device_id_type=MESH
         )
         return carry
 
-    def greet_member(k, carry):
+    def greet_member(i, carry):
+        k = lax.rem(i + nm // 2 - 2, nm - 1) + 1
         pl.semaphore_signal(
             barrier, inc=1, device_id=(lax.rem(mem + k, nm), me), device_id_type=MESH
         )
         return carry
 
-    lax.fori_loop(1, nm, greet_member, 0)
-    lax.fori_loop(1, ns, greet_space, 0)
+    lax.fori_loop(0, nm - 1, greet_member, 0)
+    lax.fori_loop(0, ns - 1, greet_space, 0)
 
     loads = [
         pltpu.make_async_copy(coarse.at[0], cs, in_sem.at[0]),
@@ -114,6 +132,61 @@
 
     def north(x, above):
         return jnp.where(rowc == rows - 1, above, roll(x, rows - 1, 0))
+
+    def cycles(full):
+        total = None
+        next_slab = jnp.minimum(me + 1, ns - 1)
+        blank = jnp.zeros((bl, 128), f32)
+        for j in range(2):
+            cw = c0[j] - 1
+            ch = c0[j] + bl
+            tw = cw >> 7
+            te = ch >> 7
+            span = pl.ds(r0[j], bl)
+            if full:
+                west_parts = [ex[3 + t, tw, span, :] for t in range(4)]
+                east_parts = [ex[t, te, span, :] for t in range(3)]
+                east_parts.append(jnp.full((bl, 128), -1.0, f32))
+            else:
+                west_parts = [ex[3, tw, span, :], ex[4, tw, span, :], blank, blank]
+                east_parts = [ex[0, te, span, :], ex[1, te, span, :], blank, blank]
+            pick_w = jnp.where((row8 == 1) & (lane8 == (cw & 127)), 1.0, 0.0)
+            pick_e = jnp.where((row8 == 0) & (lane8 == (ch & 127)), 1.0, 0.0)
+            sides = dot(pick_w, jnp.concatenate(west_parts, axis=0), NT)
+            sides = sides + dot(pick_e, jnp.concatenate(east_parts, axis=0), NT)
+            for t in range(4):
+                north_row = pl.ds(r0[j] + bl, 1)
+                south_row = pl.ds(r0[j] - 1, 1)
+                column = c0[j]
+                source = 7 + t
+                if t == 2 and not full:
+                    column = jnp.clip(anchor[1, 2 * next_slab + j], 1, cols - bl - 1)
+                    south_row = pl.ds(rows - 1, 1)
+                    source = 7
+                first = column >> 7
+                second = jnp.minimum(first + 1, cols // 128 - 1)
+                moved = []
+                for half, tile in enumerate((first, second)):
+                    if t < 2 or (t == 2 and full):
+                        rs[j, t, half, 2:3, :] = ex[t, tile, north_row, :]
+                    else:
+                        rs[j, t, half, 2:3, :] = jnp.full((1, 128), -1.0, f32)
+                    rs[j, t, half, 3:4, :] = ex[source, tile, south_row, :]
+                    moved.append(roll(rs[j, t, half], (32 * t - column) & 127, 1))
+                kept = lane8 - 32 * t < 128 - (column & 127)
+                picked = jnp.where(kept, moved[0], moved[1])
+                here = (row8 >= 2) & (row8 < 4) & (lane8 >= 32 * t) & (lane8 < 32 * t + 32)
+                sides = jnp.where(here, picked, sides)
+            sides = jnp.where(row8 < 4, sides, 0.0)
+            total = sides if j == 0 else total + roll(sides, 4, 0)
+        return total
+
+    def hold(pairs):
+        for f, held in pairs:
+            for tile in range(cols // 128):
+                ex[f, tile] = held[:, 128 * tile : 128 * tile + 128]
+
+    rs[...] = jnp.zeros(rs.shape, f32)
 
     for load in loads[:3]:
         load.wait()
@@ -139,6 +212,13 @@
     dn_s[6:7, :] = on[0:1]
     dn_s[7:8, :] = cn[0:1, :]
 
+    u1 = oe * u0 - ce[...] * (east(h1) - h1)
+    v1 = on * v0 - cn[...] * (north(h1, 0.0) - h1)
+    hold(((0, h0), (1, h1), (3, u0), (4, u1), (6, ce), (7, v0), (8, v1), (10, cn)))
+    early = cycles(False)
+    early_s[...] = early
+    early_r[ns - 1] = early
+
     pl.semaphore_wait(barrier, ns + nm - 2)
 
     up = pltpu.make_async_remote_copy(
@@ -151,13 +231,35 @@
     )
     up.start()
     down.start()
+
+    def spread_early(i, carry):
+        k = far_first(i)
+        pltpu.make_async_remote_copy(
+            src_ref=early_s, dst_ref=early_r.at[k], send_sem=send_sem.at[7],
+            recv_sem=recv_sem.at[7], device_id=(mem, lax.rem(me + k + 1, ns)),
+            device_id_type=MESH,
+        ).start()
+        return carry
+
+    lax.fori_loop(0, ns - 1, spread_early, 0)
+
+    my_patch = [slot[me * slots + s] for s in range(slots)]
+    held_parent = [p >> 1 for p in my_patch]
+
+    def find_slot(k, carry):
+        d = lax.rem(me + k + 1, ns)
+        which = jnp.int32(0)
+        for s in range(1, slots):
+            which = jnp.where(held_parent[s] == d, s, which)
+        sidx[k] = which
+        return carry
+
+    lax.fori_loop(0, ns, find_slot, 0)
 
     xb[...] = jnp.zeros(xb.shape, f32)
     gx[...] = jnp.zeros(gx.shape, f32)
     tp[...] = jnp.zeros(tp.shape, f32)
     pz[...] = jnp.zeros(pz.shape, f32)
-    rs[...] = jnp.zeros(rs.shape, f32)
-
     up.wait()
     down.wait()
 
@@ -185,50 +287,14 @@
     t2[...] = h2
     u2 = oe * u1 - ce[...] * (east(h2) - h2)
     v2 = on * v1 - cn[...] * (north(h2, h2_p) - h2)
-    for f, held in enumerate((h0, h1, h2, u0, u1, u2, ce, v0, v1, v2, cn)):
-        for tile in range(cols // 128):
-            ex[f, tile] = held[:, 128 * tile : 128 * tile + 128]
-
-    payload = None
-    for j in range(2):
-        cw = c0[j] - 1
-        ch = c0[j] + bl
-        tw = cw >> 7
-        te = ch >> 7
-        span = pl.ds(r0[j], bl)
-        west_stack = jnp.concatenate(
-            [ex[3 + t, tw, span, :] for t in range(4)], axis=0
-        )
-        east_stack = jnp.concatenate(
-            [ex[t, te, span, :] for t in range(3)] + [jnp.full((bl, 128), -1.0, f32)],
-            axis=0,
-        )
-        pick_w = jnp.where((row8 == 1) & (lane8 == (cw & 127)), 1.0, 0.0)
-        pick_e = jnp.where((row8 == 0) & (lane8 == (ch & 127)), 1.0, 0.0)
-        sides = dot(pick_w, west_stack, NT) + dot(pick_e, east_stack, NT)
-        first = c0[j] >> 7
-        second = jnp.minimum(first + 1, cols // 128 - 1)
-        north_row = pl.ds(r0[j] + bl, 1)
-        south_row = pl.ds(r0[j] - 1, 1)
-        for t in range(4):
-            moved = []
-            for half, tile in enumerate((first, second)):
-                if t < 3:
-                    rs[j, t, half, 2:3, :] = ex[t, tile, north_row, :]
-                else:
-                    rs[j, t, half, 2:3, :] = jnp.full((1, 128), -1.0, f32)
-                rs[j, t, half, 3:4, :] = ex[7 + t, tile, south_row, :]
-                moved.append(roll(rs[j, t, half], (32 * t - c0[j]) & 127, 1))
-            kept = lane8 - 32 * t < 128 - (c0[j] & 127)
-            picked = jnp.where(kept, moved[0], moved[1])
-            here = (row8 >= 2) & (row8 < 4) & (lane8 >= 32 * t) & (lane8 < 32 * t + 32)
-            sides = jnp.where(here, picked, sides)
-        sides = jnp.where(row8 < 4, sides, 0.0)
-        payload = sides if j == 0 else payload + roll(sides, 4, 0)
+    hold(((2, h2), (5, u2), (8, v1), (9, v2)))
+
+    payload = cycles(True)
     pay_s[...] = payload
     pay_r[ns - 1] = payload
 
-    def spread_payload(k, carry):
+    def spread_payload(i, carry):
+        k = far_first(i)
         pltpu.make_async_remote_copy(
             src_ref=pay_s, dst_ref=pay_r.at[k], send_sem=send_sem.at[2],
             recv_sem=recv_sem.at[2], device_id=(mem, lax.rem(me + k + 1, ns)),
@@ -237,28 +303,6 @@
         return carry
 
     lax.fori_loop(0, ns - 1, spread_payload, 0)
-
-    my_patch = [slot[me * slots + s] for s in range(slots)]
-    held_parent = [p >> 1 for p in my_patch]
-
-    def find_slot(k, carry):
-        d = lax.rem(me + k + 1, ns)
-        which = jnp.int32(0)
-        for s in range(1, slots):
-            which = jnp.where(held_parent[s] == d, s, which)
-        sidx[k] = which
-        return carry
-
-    lax.fori_loop(0, ns, find_slot, 0)
-
-    def find_owner(i, carry):
-        p = slot[i]
-        return tuple(
-            jnp.where(p == 2 * me + j, i, carry[j]) for j in range(2)
-        )
-
-    where_held = lax.fori_loop(0, ns * slots, find_owner, (jnp.int32(0), jnp.int32(0)))
-    owner_at = [lax.rem(me - w // slots - 1 + 2 * ns, ns) for w in where_held]
 
     def all_of(ref, count, sem):
         part = ref.at[pl.ds(0, count)]
@@ -295,8 +339,8 @@
 
     def expand(old, diff):
         both = jnp.concatenate([old, diff], axis=0)
-        ycol[:, 0 : 2 * nb] = dot(spread_rows, both, NT)
-        yrow[...] = dot(both, spread_lanes)
+        ycol[:, 0 : 2 * nb] = dot3_nt(spread_rows, both)
+        yrow[...] = dot3(both, spread_lanes)
         for s in range(slots):
             eo[s] = roll(ycol[...], 127 - 8 * s, 1)
             ed[s] = roll(ycol[...], (255 - 8 * s - nb) % 128, 1)
@@ -369,13 +413,23 @@
 
     for load in loads[3:]:
         load.wait()
-    all_of(pay_r, ns - 1, recv_sem.at[2])
-
+    def take(held, s, rows_from, count, slab):
+        at = lax.rem(me - slab - 1 + 2 * ns, ns)
+        p = jnp.maximum(my_patch[s], 0)
+        got = held[at, pl.ds((p & 1) * 4 + rows_from, count), :]
+        return jnp.where(my_patch[s] >= 0, got, 0.0)
+
+    all_of(early_r, ns - 1, recv_sem.at[7])
     for s in range(slots):
         p = jnp.maximum(my_patch[s], 0)
-        at = lax.rem(me - (p >> 1) - 1 + 2 * ns, ns)
-        got = pay_r[at, pl.ds((p & 1) * 4, 4), :]
-        xb[8 * s : 8 * s + 4, :] = jnp.where(my_patch[s] >= 0, got, 0.0)
+        parent = p >> 1
+        got = take(early_r, s, 0, 4, parent)
+        lower = take(early_r, s, 3, 1, jnp.maximum(parent - 1, 0))
+        mine = got[3:4]
+        fix = C * roll(mine, 64, 1) * roll(lower, 96, 1)
+        fixed = (lane >= 32) & (lane < 64) & (anchor[0, p] == 1) & (parent > 0)
+        xb[8 * s : 8 * s + 3, :] = got[0:3]
+        xb[8 * s + 3 : 8 * s + 4, :] = jnp.where(fixed, mine + fix, mine)
 
     x = xb[...]
     left = lane_nb < 32
@@ -394,7 +448,7 @@
     for s in range(slots):
         tp[s, 64:96, :] = mean[bl * s : bl * s + bl]
     for s in range(slots):
-        side = dot(pick, tp[s], NT)
+        side = dot3_nt(pick, tp[s])
         side = side[0:8] + roll(side[8:16], 1, 1)
         gx[8 * s : 8 * s + 2, :] = side[0:2]
         top = tp[s, 95:96, :]
@@ -403,6 +457,10 @@
         gx[8 * s + 3 : 8 * s + 4, :] = roll(low_row, 64, 1) - C * (
             roll(low_row, 32, 1) - jnp.where(lane > 64, roll(low_row, 33, 1), 0.0) + low_row
         )
+    all_of(pay_r, ns - 1, recv_sem.at[2])
+    for s in range(slots):
+        xb[8 * s : 8 * s + 4, :] = take(pay_r, s, 0, 4, jnp.maximum(my_patch[s], 0) >> 1)
+    x = xb[...]
     new = x - roll(x, 96, 1) * gx[...]
     mid = (lane_nb >= 64) & (lane_nb < 96)
     expand(
@@ -435,7 +493,8 @@
     value = outside + jnp.sum(jnp.where(at_row, found, 0.0), axis=0, keepdims=True)
     z_s[0] = value
 
-    def send_member(k, carry):
+    def send_member(i, carry):
+        k = lax.rem(i + nm // 2 - 2, nm - 1)
         pltpu.make_async_remote_copy(
             src_ref=z_s.at[0], dst_ref=z_r.at[k], send_sem=send_sem.at[5],
             recv_sem=recv_sem.at[5], device_id=(lax.rem(mem + k + 1, nm), me),
@@ -452,7 +511,8 @@
                 lane8 < 96, piece, roll(tail, 96 - 32 * i, 1)
             )
 
-    def send_mean(k, carry):
+    def send_mean(i, carry):
+        k = far_first(i)
         a2_s[k] = a2_p[sidx[k]]
         pltpu.make_async_remote_copy(
             src_ref=a2_s.at[k], dst_ref=a2_r.at[k], send_sem=send_sem.at[4],
@@ -472,7 +532,8 @@
     for s in range(slots):
         m1_p[s] = jnp.sum(packed[8 * s : 8 * s + 8], axis=0, keepdims=True)
 
-    def send_cycle(k, carry):
+    def send_cycle(i, carry):
+        k = far_first(i)
         m1_s[k] = m1_p[sidx[k]]
         pltpu.make_async_remote_copy(
             src_ref=m1_s.at[k], dst_ref=m1_r.at[k], send_sem=send_sem.at[3],
@@ -494,7 +555,8 @@
         center = center + weight(lax.rem(mem - k - 1 + nm, nm)) * z_r[k]
     g_s[0] = value - center
 
-    def send_gauge(k, carry):
+    def send_gauge(i, carry):
+        k = far_first(i)
         pltpu.make_async_remote_copy(
             src_ref=g_s.at[0], dst_ref=g_r.at[k], send_sem=send_sem.at[6],
             recv_sem=recv_sem.at[6], device_id=(mem, lax.rem(me + k + 1, ns)),
@@ -503,6 +565,15 @@
         return carry
 
     lax.fori_loop(0, ns - 1, send_gauge, 0)
+
+    def find_owner(i, carry):
+        p = slot[i]
+        return tuple(
+            jnp.where(p == 2 * me + j, i, carry[j]) for j in range(2)
+        )
+
+    where_held = lax.fori_loop(0, ns * slots, find_owner, (jnp.int32(0), jnp.int32(0)))
+    owner_at = [lax.rem(me - w // slots - 1 + 2 * ns, ns) for w in where_held]
 
     all_of(m1_r, ns - 1, recv_sem.at[3])
     rowh = iota((rows, 128), 0)
@@ -562,6 +633,7 @@
         total = total + g_r[k]
     spread_out[...] = total
 
+    all_of(early_r, ns - 1, send_sem.at[7])
     all_of(pay_r, ns - 1, send_sem.at[2])
     all_of(m1_r, ns - 1, send_sem.at[3])
     all_of(a2_r, ns - 1, send_sem.at[4])
@@ -607,7 +679,8 @@
             buf(slots, fl + 16, fl), buf(slots, fl, fl), buf(slots, fl + 16, fl),
             buf(slots, fl, fl), buf(slots, fl, 128), buf(slots, fl, 128),
             buf(8, cols), buf(8, cols), buf(8, cols), buf(8, cols),
-            buf(2, 4, 2, 8, 128), buf(8, 128), buf(ns, 8, 128), buf(nb, 128), buf(nb, 128),
+            buf(2, 4, 2, 8, 128), buf(8, 128), buf(ns, 8, 128),
+            buf(8, 128), buf(ns, 8, 128), buf(nb, 128), buf(nb, 128),
             buf(fl, 128), buf(2 * nb, 128), buf(3, slots * fl // REFINE, 128),
             buf(slots, 128, 128),
             buf(slots, 1, 128), buf(ns, 1, 128), buf(ns, 1, 128),
@@ -615,8 +688,8 @@
             buf(2, 128, 128),
             buf(1, 1, 128), buf(nm, 1, 128), buf(1, 1, 128), buf(ns, 1, 128),
             pltpu.SMEM((ns,), jnp.int32),
-            pltpu.SemaphoreType.DMA((7,)), pltpu.SemaphoreType.DMA((7,)),
-            pltpu.SemaphoreType.DMA((7,)),
+            pltpu.SemaphoreType.DMA((7,)), pltpu.SemaphoreType.DMA((8,)),
+            pltpu.SemaphoreType.DMA((8,)),
         ],
         compiler_params=pltpu.CompilerParams(
             collective_id=0, has_side_effects=True, vmem_limit_bytes=56 * 1024 * 1024

time: 45.7 us -> 42.4 us (0.928)
  Pallas kernels: 44.9 us -> 41.6 us
    pallas_call x1, Pallas kernels: 43.8 us -> 40.4 us  [shards(): pl.pallas_call(functools.partial(kernel, ns, nm, slots), out_shape=tuple(...]
where the time goes in v4:
time: 42.4 us; the launch traced here: 42.2 us
  Pallas kernels  41.6 us (98%)
  between operations  0.64 us (2%)
    pallas_call x1, Pallas kernels, shards(): pl.pallas_call(functools.partial(kernel, ns, nm, slots), out_shape=tuple(...  40.4 us
    pallas_call x1, Pallas kernels, shards(): pl.pallas_call(store_results, out_shape=tuple((jax.ShapeDtypeStruct(shape...  1.17 us

profile of v4, /device:TPU:1, one launch (start us, length us, event | category | flops | bytes accessed | tf_op | source)
XLA Modules:
  0.0 42.2 jit_solution(7581688108846757222)
XLA Ops:
  0.6 40.4 %shard_map.103 = (f32[1,3,64,512]{3,2,1,0:T(8,128)S(1)}, f32[1,3,6,128,128]{4,3,2,1,0:T(8,128)S(1)}, f32[1,128]{1,0:T(1,128)S(1)}) custom-call(s32[192]{0:T(256)} %slot.1, s32[2,64]{1,0:T(2,128)} %bitcast.2, s32[1,128]{1,0:T(1,128)} %bitcast.3, f32[1,3,64,512]{3,2,1,0:T(8,128)} %coarse.1, f32[64,512]{1,0:T(8,128)} %seabed.1, s32[2,64,512]{2,1,0:T(8,128)} %faces.1, ...), custom_call_target="tpu_custom_call" | custom-call | tf_op jit(solution)/shard_map/pallas_call | solution.py:670
  41.1 1.2 %shard_map.104 = (f32[1,3,64,512]{3,2,1,0:T(8,128)}, f32[1,3,6,128,128]{4,3,2,1,0:T(8,128)}, f32[1,128]{1,0:T(1,128)}) custom-call(f32[1,3,64,512]{3,2,1,0:T(8,128)S(1)} %get-tuple-element.6.coarse, f32[1,3,6,128,128]{4,3,2,1,0:T(8,128)S(1)} %get-tuple-element.7.fine, f32[1,128]{1,0:T(1,128)S(1)} %get-tuple-element.8.spread), custom_call_target="tpu_custom_call" | custom-call | tf_op jit(solution)/shard_map/pallas_call | solution.py:702

commit v5 on v4

--- a/solution.py
+++ b/solution.py
@@ -13,12 +13,6 @@
 f32 = jnp.float32
 NT = (((1,), (1,)), ((), ()))
 NN = (((1,), (0,)), ((), ()))
-
-
-def dot(a, b, dims=NN):
-    return lax.dot_general(
-        a, b, dims, precision=lax.Precision.HIGHEST, preferred_element_type=f32
-    )
 
 
 def terms(x):
@@ -100,7 +94,7 @@
         pltpu.make_async_copy(fine.at[0, 2], fv.at[:, pl.ds(8, fl), :], in_sem.at[5]),
         pltpu.make_async_copy(fseabed, fd, in_sem.at[6]),
     ]
-    for load in loads:
+    for load in loads[:3]:
         load.start()
 
     r0 = [jnp.clip(anchor[0, 2 * me + j], 1, rows - bl - 1) for j in range(2)]
@@ -133,7 +127,10 @@
     def north(x, above):
         return jnp.where(rowc == rows - 1, above, roll(x, rows - 1, 0))
 
-    def cycles(full):
+    pick_row = iota((16, 256), 0)
+    pick_lane = iota((16, 256), 1)
+
+    def cycles(times):
         total = None
         next_slab = jnp.minimum(me + 1, ns - 1)
         blank = jnp.zeros((bl, 128), f32)
@@ -143,23 +140,24 @@
             tw = cw >> 7
             te = ch >> 7
             span = pl.ds(r0[j], bl)
-            if full:
-                west_parts = [ex[3 + t, tw, span, :] for t in range(4)]
-                east_parts = [ex[t, te, span, :] for t in range(3)]
-                east_parts.append(jnp.full((bl, 128), -1.0, f32))
-            else:
-                west_parts = [ex[3, tw, span, :], ex[4, tw, span, :], blank, blank]
-                east_parts = [ex[0, te, span, :], ex[1, te, span, :], blank, blank]
-            pick_w = jnp.where((row8 == 1) & (lane8 == (cw & 127)), 1.0, 0.0)
-            pick_e = jnp.where((row8 == 0) & (lane8 == (ch & 127)), 1.0, 0.0)
-            sides = dot(pick_w, jnp.concatenate(west_parts, axis=0), NT)
-            sides = sides + dot(pick_e, jnp.concatenate(east_parts, axis=0), NT)
+            level = jnp.full((bl, 128), -1.0, f32)
+            west_parts = [ex[3 + t, tw, span, :] if t in times else blank for t in range(4)]
+            east_parts = [ex[t, te, span, :] if t in times else blank for t in range(3)]
+            east_parts.append(level if 3 in times else blank)
+            at_west = (pick_row == 1) & (pick_lane == (cw & 127))
+            at_east = (pick_row == 0) & (pick_lane == 128 + (ch & 127))
+            both = jnp.concatenate(
+                [jnp.concatenate(parts, axis=0) for parts in (west_parts, east_parts)], axis=1
+            )
+            sides = dot3_nt(jnp.where(at_west | at_east, 1.0, 0.0), both)[0:8]
             for t in range(4):
+                if t not in times and 2 in times:
+                    continue
                 north_row = pl.ds(r0[j] + bl, 1)
                 south_row = pl.ds(r0[j] - 1, 1)
                 column = c0[j]
                 source = 7 + t
-                if t == 2 and not full:
+                if t not in times:
                     column = jnp.clip(anchor[1, 2 * next_slab + j], 1, cols - bl - 1)
                     south_row = pl.ds(rows - 1, 1)
                     source = 7
@@ -167,7 +165,7 @@
                 second = jnp.minimum(first + 1, cols // 128 - 1)
                 moved = []
                 for half, tile in enumerate((first, second)):
-                    if t < 2 or (t == 2 and full):
+                    if t in times and t < 3:
                         rs[j, t, half, 2:3, :] = ex[t, tile, north_row, :]
                     else:
                         rs[j, t, half, 2:3, :] = jnp.full((1, 128), -1.0, f32)
@@ -190,6 +188,8 @@
 
     for load in loads[:3]:
         load.wait()
+    for load in loads[3:]:
+        load.start()
     h0, u0, v0 = cs[0], cs[1], cs[2]
     oe = op[0].astype(f32)
     on = op[1].astype(f32)
@@ -197,7 +197,6 @@
     ce[...] = cd * oe
     cn[...] = cd * on
     h1 = h0 - C * (u0 - west(u0) + v0 - south(v0, 0.0))
-    t1[0] = h1
     up_s[0:1, :] = h1[rows - 1 : rows]
     up_s[1:2, :] = v0[rows - 1 : rows]
     up_s[2:3, :] = on[rows - 1 : rows]
@@ -214,8 +213,17 @@
 
     u1 = oe * u0 - ce[...] * (east(h1) - h1)
     v1 = on * v0 - cn[...] * (north(h1, 0.0) - h1)
-    hold(((0, h0), (1, h1), (3, u0), (4, u1), (6, ce), (7, v0), (8, v1), (10, cn)))
-    early = cycles(False)
+    t1[0] = h1
+    h1 = jnp.where(block, 0.0, h1)
+    u1 = jnp.where(block, 0.0, u1)
+    v1 = jnp.where(block, 0.0, v1)
+    h2 = h1 - C * (u1 - west(u1) + v1 - south(v1, 0.0))
+    t1[1], t1[2], t2[...] = u1, v1, h2
+    u2 = oe * u1 - ce[...] * (east(h2) - h2)
+    v2 = on * v1 - cn[...] * (north(h2, 0.0) - h2)
+    hold(((0, h0), (1, h1), (2, h2), (3, u0), (4, u1), (5, u2), (6, ce)))
+    hold(((7, v0), (8, v1), (9, v2), (10, cn)))
+    early = cycles((0, 1, 3))
     early_s[...] = early
     early_r[ns - 1] = early
 
@@ -263,33 +271,70 @@
     up.wait()
     down.wait()
 
+    strip_row = iota((8, cols), 0)
+    strip_lane = iota((8, cols), 1)
+
+    def strip(o):
+        inside = None
+        for j in range(2):
+            hit = (
+                (strip_row + o >= r0[j]) & (strip_row + o < r0[j] + bl)
+                & (strip_lane >= c0[j]) & (strip_lane < c0[j] + bl)
+            )
+            inside = hit if inside is None else inside | hit
+        part = slice(o, o + 8)
+        faces_here = (op[0, part, :].astype(f32), op[1, part, :].astype(f32))
+        return inside, part, faces_here
+
+    def strip_south(x, below):
+        return jnp.where(strip_row == 0, below, roll(x, 1, 0))
+
+    def strip_north(x, above):
+        return jnp.where(strip_row == 7, above, roll(x, 7, 0))
+
+    def renew(o, h, below_of, above, above2_of):
+        inside, part, (oe_s, on_s) = strip(o)
+        ce_s, cn_s = ce[part, :], cn[part, :]
+        u = oe_s * cs[1, part, :] - ce_s * (east(h) - h)
+        v = on_s * cs[2, part, :] - cn_s * (strip_north(h, above) - h)
+        below = below_of(h)
+        above2 = above2_of(v)
+        hm = jnp.where(inside, 0.0, h)
+        um = jnp.where(inside, 0.0, u)
+        vm = jnp.where(inside, 0.0, v)
+        second = hm - C * (um - west(um) + vm - strip_south(vm, below))
+        u2 = oe_s * um - ce_s * (east(second) - second)
+        v2 = on_s * vm - cn_s * (strip_north(second, above2) - second)
+        t1[1, part, :], t1[2, part, :], t2[part, :] = um, vm, second
+        for f, held in ((2, second), (5, u2), (8, vm), (9, v2)):
+            for tile in range(cols // 128):
+                ex[f, tile, part, :] = held[:, 128 * tile : 128 * tile + 128]
+        return above2
+
     low = me > 0
     high = me < ns - 1
     h1_m = up_r[0:1, :]
     v0_m = jnp.where(low, up_r[1:2, :], 0.0)
-    h1 = jnp.where(rowc == 0, h1 + C * v0_m, h1)
-    h1_p = jnp.where(high, dn_r[0:1, :] + C * v0[rows - 1 : rows], 0.0)
-    u1 = oe * u0 - ce[...] * (east(h1) - h1)
-    v1 = on * v0 - cn[...] * (north(h1, h1_p) - h1)
+    v0_top = cs[2, rows - 1 : rows, :]
+    h1_p = jnp.where(high, dn_r[0:1, :] + C * v0_top, 0.0)
     u1_p = dn_r[4:5, :] * dn_r[1:2, :] - dn_r[5:6, :] * (east(h1_p) - h1_p)
     v1_p = dn_r[6:7, :] * dn_r[2:3, :] - dn_r[7:8, :] * (dn_r[3:4, :] - h1_p)
-    v1_m = jnp.where(
-        low, up_r[2:3, :] * v0_m - up_r[3:4, :] * (h1[0:1] - h1_m), 0.0
-    )
-    h2_p = jnp.where(
-        high, h1_p - C * (u1_p - west(u1_p) + v1_p - v1[rows - 1 : rows]), 0.0
-    )
-    h1 = jnp.where(block, 0.0, h1)
-    u1 = jnp.where(block, 0.0, u1)
-    v1 = jnp.where(block, 0.0, v1)
-    h2 = h1 - C * (u1 - west(u1) + v1 - south(v1, v1_m))
-    t1[0], t1[1], t1[2] = h1, u1, v1
-    t2[...] = h2
-    u2 = oe * u1 - ce[...] * (east(h2) - h2)
-    v2 = on * v1 - cn[...] * (north(h2, h2_p) - h2)
-    hold(((2, h2), (5, u2), (8, v1), (9, v2)))
-
-    payload = cycles(True)
+
+    def below_first(h):
+        return jnp.where(low, up_r[2:3, :] * v0_m - up_r[3:4, :] * (h[0:1] - h1_m), 0.0)
+
+    def above_last(v):
+        return jnp.where(high, h1_p - C * (u1_p - west(u1_p) + v1_p - v[7:8]), 0.0)
+
+    h_low = t1[0, 0:8, :]
+    h_low = jnp.where(strip_row == 0, h_low + C * v0_m, h_low)
+    above_low = t1[0, 8:9, :]
+    second_above_low = t2[8:9, :]
+    below_high = t1[2, rows - 9 : rows - 8, :]
+    renew(0, h_low, below_first, above_low, lambda v: second_above_low)
+    h2_p = renew(rows - 8, t1[0, rows - 8 : rows, :], lambda h: below_high, h1_p, above_last)
+
+    payload = cycles((2,))
     pay_s[...] = payload
     pay_r[ns - 1] = payload
 
@@ -322,7 +367,7 @@
         )
         covered = hit if covered is None else covered | hit
     pick_col = jnp.where(iota((cols, 128), 0) == gcol, 1.0, 0.0)
-    found = dot3(h2, pick_col)
+    found = dot3(t2[...], pick_col)
     outside = jnp.sum(
         jnp.where((iota((rows, 128), 0) == own_row) & jnp.logical_not(covered), found, 0.0),
         axis=0, keepdims=True,
@@ -389,7 +434,7 @@
             update(k, False)
             return carry
 
-        lax.fori_loop(0, REFINE - 1 if last else REFINE, step, 0)
+        lax.fori_loop(0, REFINE - 1 if last else REFINE, step, 0, unroll=True)
         if last:
             update(jnp.int32(REFINE - 1), True)
 
@@ -458,11 +503,11 @@
             roll(low_row, 32, 1) - jnp.where(lane > 64, roll(low_row, 33, 1), 0.0) + low_row
         )
     all_of(pay_r, ns - 1, recv_sem.at[2])
+    mid = (lane_nb >= 64) & (lane_nb < 96)
     for s in range(slots):
         xb[8 * s : 8 * s + 4, :] = take(pay_r, s, 0, 4, jnp.maximum(my_patch[s], 0) >> 1)
-    x = xb[...]
+    x = jnp.where(mid, xb[...], x)
     new = x - roll(x, 96, 1) * gx[...]
-    mid = (lane_nb >= 64) & (lane_nb < 96)
     expand(
         jnp.where((lane_nb >= 32) & (lane_nb < 64), x, 0.0),
         jnp.where(mid, new - roll(x, 32, 1), 0.0),

time: 42.4 us -> 41.7 us (0.983)
  Pallas kernels: 41.6 us -> 40.9 us
    pallas_call x1, Pallas kernels: 40.4 us -> 39.7 us  [shards(): pl.pallas_call(functools.partial(kernel, ns, nm, slots), out_shape=tuple(...]
where the time goes in v5:
time: 41.7 us; the launch traced here: 41.5 us
  Pallas kernels  40.9 us (98%)
  between operations  0.64 us (2%)
    pallas_call x1, Pallas kernels, shards(): pl.pallas_call(functools.partial(kernel, ns, nm, slots), out_shape=tuple(...  39.7 us
    pallas_call x1, Pallas kernels, shards(): pl.pallas_call(store_results, out_shape=tuple((jax.ShapeDtypeStruct(shape...  1.17 us

profile of v5, /device:TPU:1, one launch (start us, length us, event | category | flops | bytes accessed | tf_op | source)
XLA Modules:
  0.0 41.5 jit_solution(5289377644802529002)
XLA Ops:
  0.6 39.7 %shard_map.103 = (f32[1,3,64,512]{3,2,1,0:T(8,128)S(1)}, f32[1,3,6,128,128]{4,3,2,1,0:T(8,128)S(1)}, f32[1,128]{1,0:T(1,128)S(1)}) custom-call(s32[192]{0:T(256)} %slot.1, s32[2,64]{1,0:T(2,128)} %bitcast.2, s32[1,128]{1,0:T(1,128)} %bitcast.3, f32[1,3,64,512]{3,2,1,0:T(8,128)} %coarse.1, f32[64,512]{1,0:T(8,128)} %seabed.1, s32[2,64,512]{2,1,0:T(8,128)} %faces.1, ...), custom_call_target="tpu_custom_call" | custom-call | tf_op jit(solution)/shard_map/pallas_call | solution.py:715
  40.4 1.2 %shard_map.104 = (f32[1,3,64,512]{3,2,1,0:T(8,128)}, f32[1,3,6,128,128]{4,3,2,1,0:T(8,128)}, f32[1,128]{1,0:T(1,128)}) custom-call(f32[1,3,64,512]{3,2,1,0:T(8,128)S(1)} %get-tuple-element.6.coarse, f32[1,3,6,128,128]{4,3,2,1,0:T(8,128)S(1)} %get-tuple-element.7.fine, f32[1,128]{1,0:T(1,128)S(1)} %get-tuple-element.8.spread), custom_call_target="tpu_custom_call" | custom-call | tf_op jit(solution)/shard_map/pallas_call | solution.py:747

commit v6 on v5

--- a/solution.py
+++ b/solution.py
@@ -82,8 +82,8 @@
         )
         return carry
 
-    lax.fori_loop(0, nm - 1, greet_member, 0)
-    lax.fori_loop(0, ns - 1, greet_space, 0)
+    lax.fori_loop(0, nm - 1, greet_member, 0, unroll=True)
+    lax.fori_loop(0, ns - 1, greet_space, 0, unroll=True)
 
     loads = [
         pltpu.make_async_copy(coarse.at[0], cs, in_sem.at[0]),
@@ -249,7 +249,7 @@
         ).start()
         return carry
 
-    lax.fori_loop(0, ns - 1, spread_early, 0)
+    lax.fori_loop(0, ns - 1, spread_early, 0, unroll=True)
 
     my_patch = [slot[me * slots + s] for s in range(slots)]
     held_parent = [p >> 1 for p in my_patch]
@@ -347,7 +347,7 @@
         ).start()
         return carry
 
-    lax.fori_loop(0, ns - 1, spread_payload, 0)
+    lax.fori_loop(0, ns - 1, spread_payload, 0, unroll=True)
 
     def all_of(ref, count, sem):
         part = ref.at[pl.ds(0, count)]
@@ -547,7 +547,7 @@
         ).start()
         return carry
 
-    lax.fori_loop(0, nm - 1, send_member, 0)
+    lax.fori_loop(0, nm - 1, send_member, 0, unroll=True)
     for s in range(slots):
         tail = mean[bl * s + 24 : bl * s + 32]
         for i in range(3):
@@ -590,14 +590,15 @@
     lax.fori_loop(0, ns - 1, send_cycle, 0)
     m1_r[ns - 1] = m1_p[sidx[ns - 1]]
 
-    all_of(z_r, nm - 1, recv_sem.at[5])
-
     def weight(m):
         return (1.0 + 2.0 * m.astype(f32) / (nm - 1)) / (2.0 * nm)
 
+    weights = [weight(lax.rem(mem - k - 1 + nm, nm)) for k in range(nm - 1)]
     center = weight(mem) * value
+    all_of(z_r, nm - 1, recv_sem.at[5])
+
     for k in range(nm - 1):
-        center = center + weight(lax.rem(mem - k - 1 + nm, nm)) * z_r[k]
+        center = center + weights[k] * z_r[k]
     g_s[0] = value - center
 
     def send_gauge(i, carry):
@@ -609,7 +610,7 @@
         ).start()
         return carry
 
-    lax.fori_loop(0, ns - 1, send_gauge, 0)
+    lax.fori_loop(0, ns - 1, send_gauge, 0, unroll=True)
 
     def find_owner(i, carry):
         p = slot[i]

time: 41.7 us -> 41.2 us (0.988)
  Pallas kernels: 40.9 us -> 40.4 us
    pallas_call x1, Pallas kernels: 39.7 us -> 39.2 us  [shards(): pl.pallas_call(functools.partial(kernel, ns, nm, slots), out_shape=tuple(...]
where the time goes in v6:
time: 41.2 us; the launch traced here: 41 us
  Pallas kernels  40.4 us (98%)
  between operations  0.64 us (2%)
    pallas_call x1, Pallas kernels, shards(): pl.pallas_call(functools.partial(kernel, ns, nm, slots), out_shape=tuple(...  39.2 us
    pallas_call x1, Pallas kernels, shards(): pl.pallas_call(store_results, out_shape=tuple((jax.ShapeDtypeStruct(shape...  1.17 us

profile of v6, /device:TPU:1, one launch (start us, length us, event | category | flops | bytes accessed | tf_op | source)
XLA Modules:
  0.0 41.0 jit_solution(11069028214946673432)
XLA Ops:
  0.6 39.2 %shard_map.103 = (f32[1,3,64,512]{3,2,1,0:T(8,128)S(1)}, f32[1,3,6,128,128]{4,3,2,1,0:T(8,128)S(1)}, f32[1,128]{1,0:T(1,128)S(1)}) custom-call(s32[192]{0:T(256)} %slot.1, s32[2,64]{1,0:T(2,128)} %bitcast.2, s32[1,128]{1,0:T(1,128)} %bitcast.3, f32[1,3,64,512]{3,2,1,0:T(8,128)} %coarse.1, f32[64,512]{1,0:T(8,128)} %seabed.1, s32[2,64,512]{2,1,0:T(8,128)} %faces.1, ...), custom_call_target="tpu_custom_call" | custom-call | tf_op jit(solution)/shard_map/pallas_call | solution.py:716
  39.8 1.2 %shard_map.104 = (f32[1,3,64,512]{3,2,1,0:T(8,128)}, f32[1,3,6,128,128]{4,3,2,1,0:T(8,128)}, f32[1,128]{1,0:T(1,128)}) custom-call(f32[1,3,64,512]{3,2,1,0:T(8,128)S(1)} %get-tuple-element.6.coarse, f32[1,3,6,128,128]{4,3,2,1,0:T(8,128)S(1)} %get-tuple-element.7.fine, f32[1,128]{1,0:T(1,128)S(1)} %get-tuple-element.8.spread), custom_call_target="tpu_custom_call" | custom-call | tf_op jit(solution)/shard_map/pallas_call | solution.py:748
